TPU v7x, 32 devices: a whole 2x2x4 slice. The times are simulated.
32 devices in a mesh: dp: 8 (over z, core), shard: 4 (over y, x).
Axes of the slice: x: 2, y: 2, z: 4, core: 2. Of those that a mesh axis runs over, the one named last changes fastest.
Arguments:
- queries: float32 [16384, 256], P(('dp', 'shard'))
- items: float32 [81920, 256], P('shard')
- positive: int32 [16384], P(('dp', 'shard')), may hold values from 0 to 81919
- tile_ids: int32 [32, 4, 3], P(('dp', 'shard')), may hold values from 0 to 39, as said below
- counts: int32 [32, 4], P(('dp', 'shard')), may hold values from 1 to 3, as said below
Outputs:
- loss: float32 [16384], P(('dp', 'shard'))
- query_grad: float32 [16384, 256], P(('dp', 'shard'))
- item_grad: float32 [81920, 256], P(('shard', 'dp'))
Inputs may be any that keep to these rules, and one draw needn't show every extreme that they name: `tile_ids`: within one block and shard the 3 entries are distinct; only the first counts of them are visited. `counts`: every block visits exactly 3 tiles on at least one shard.
All inputs are finite; a program needn't handle non-finite values.
Results may differ from a plain program's by a relative error of at most 0.0003.
Values sent between devices are 32-bit elements; how exact they have to be, the bound alone decides.
No kernel may reach another device: no remote copies, remote signals or barrier semaphores. Data moves between devices by JAX's collectives and lax.ppermute only.
A program may use at most 192 MiB of HBM per device.

v0:
```python
import jax
import jax.numpy as jnp
from jax import lax
from jax.sharding import PartitionSpec as P

TILE = 512


very_low = -1e30


def joined(part, axis, combine):
    gathered = jax.tree.map(lambda a: lax.all_gather(a, axis), part)

    def take(source):
        return jax.tree.map(lambda a: lax.dynamic_index_in_dim(a, source, 0, False), gathered)

    return lax.fori_loop(
        1, lax.axis_size(axis), lambda source, state: combine(state, take(source)), take(0)
    )


def positive_row(qblk, pblk, items, shard_at):
    local_rows = items.shape[0]
    offset = pblk - shard_at * local_rows
    inside = (offset >= 0) & (offset < local_rows)
    safe = jnp.clip(offset, 0, local_rows - 1)
    target = jnp.where(inside, offset, local_rows)
    chosen = jnp.take(items, safe, axis=0)
    logit = jnp.where(inside, jnp.sum(qblk * chosen, axis=1), 0.0)
    return (inside, target, chosen, logit)


def tile_logits(qblk, items, tile):
    block = lax.dynamic_slice_in_dim(items, tile * TILE, TILE, 0)
    logits = jnp.einsum(
        "qd,td->qt",
        qblk,
        block,
        precision=lax.Precision.HIGHEST,
        preferred_element_type=jnp.float32,
    )
    return (logits, block)


def block_stats(qblk, pblk, idrow, count, items, shard_at):
    rows = qblk.shape[0]

    def visit(step, carry):
        top, total = carry
        logits, block = tile_logits(qblk, items, idrow[step])
        new_top = jnp.maximum(top, jnp.max(logits, axis=1))
        total = total * jnp.exp(top - new_top) + jnp.sum(jnp.exp(logits - new_top[:, None]), axis=1)
        return (new_top, total)

    start = (jnp.full((rows,), very_low, jnp.float32), jnp.zeros((rows,), jnp.float32))
    top, total = lax.fori_loop(0, count, visit, start)
    inside, target, chosen, logit = positive_row(qblk, pblk, items, shard_at)
    new_top = jnp.maximum(top, jnp.where(inside, logit, very_low))
    total = total * jnp.exp(top - new_top) + jnp.where(inside, jnp.exp(logit - new_top), 0.0)
    return ((new_top, total, logit), (inside, target, chosen))


def block_grads(qblk, idrow, count, lse, items, d_local, inside, chosen, plogit):
    high = lax.Precision.HIGHEST

    def visit(step, carry):
        dq, grads = carry
        tile = idrow[step]
        logits, block = tile_logits(qblk, items, tile)
        prob = jnp.exp(logits - lse[:, None])
        dq = dq + jnp.dot(prob, block, precision=high, preferred_element_type=jnp.float32)
        update = jnp.einsum(
            "qt,qd->td", prob, qblk, precision=high, preferred_element_type=jnp.float32
        )
        current = lax.dynamic_slice_in_dim(grads, tile * TILE, TILE, 0)
        grads = lax.dynamic_update_slice_in_dim(grads, current + update, tile * TILE, 0)
        return (dq, grads)

    dq, d_local = lax.fori_loop(0, count, visit, (jnp.zeros(qblk.shape, jnp.float32), d_local))
    weight = jnp.where(inside, jnp.exp(plogit - lse) - 1.0, 0.0)
    dq = dq + weight[:, None] * chosen
    return (dq, d_local, weight[:, None] * qblk)


def combine_stats(first, second):
    top = jnp.maximum(first[0], second[0])
    total = first[1] * jnp.exp(first[0] - top) + second[1] * jnp.exp(second[0] - top)
    return (top, total, first[2] + second[2])


def local(queries, items, positive, tile_ids, counts):
    shard_at = lax.axis_index("shard")
    n_shard = lax.axis_size("shard")
    rows = queries.shape[0]
    width = queries.shape[1]
    seen_q, seen_pos, seen_ids, seen_cnt = (
        lax.all_gather(queries, "shard", axis=0, tiled=True),
        lax.all_gather(positive, "shard", axis=0, tiled=True),
        lax.all_gather(tile_ids, "shard", axis=0, tiled=True),
        lax.all_gather(counts, "shard", axis=0, tiled=True),
    )
    seen_q = seen_q.reshape(n_shard, rows, width)
    seen_pos = seen_pos.reshape(n_shard, rows)
    idrows = jnp.take(seen_ids, shard_at, axis=1)
    seen_counts = jnp.take(seen_cnt, shard_at, axis=1)

    def stats_of(xs):
        return block_stats(xs[0], xs[1], xs[2], xs[3], items, shard_at)

    (tops, totals, plogs), (insides, targets, chosens) = lax.map(
        stats_of, (seen_q, seen_pos, idrows, seen_counts)
    )
    local_plogs = plogs
    tops, totals, plogs = joined((tops, totals, plogs), "shard", combine_stats)
    lse = tops + jnp.log(totals)
    loss = jnp.take(lse, shard_at, axis=0) - jnp.take(plogs, shard_at, axis=0)
    d_local = jnp.zeros(items.shape, jnp.float32)

    def grads_of(grads, xs):
        dq, grads, update = block_grads(
            xs[0], xs[1], xs[2], xs[3], items, grads, xs[4], xs[5], xs[6]
        )
        return (grads, (dq, update))

    d_local, (dq_parts, updates) = lax.scan(
        grads_of, d_local, (seen_q, idrows, seen_counts, lse, insides, chosens, local_plogs)
    )
    d_local = d_local.at[targets.reshape(-1)].add(updates.reshape(-1, width), mode="drop")
    query_grad = lax.psum_scatter(dq_parts, "shard", scatter_dimension=0, tiled=True).reshape(
        rows, width
    )
    item_grad = lax.psum_scatter(d_local, "dp", scatter_dimension=0, tiled=True)
    return (loss, query_grad, item_grad)


def solution(mesh):
    placed = (
        P(("dp", "shard"), None),
        P("shard", None),
        P(("dp", "shard")),
        P(("dp", "shard"), None, None),
        P(("dp", "shard"), None),
    )
    return jax.shard_map(
        local,
        mesh=mesh,
        in_specs=placed,
        out_specs=(P(("dp", "shard")), P(("dp", "shard"), None), P(("shard", "dp"), None)),
        check_vma=False,
    )
```

profile of v0, /device:TPU:0, one launch (start us, length us, event | category | flops | bytes accessed | tf_op | source)
XLA Modules:
  0.0 549.2 jit_solution(11068130729784273246)
XLA Ops:
  8.7 9.5 %all-gather.3 = s32[4,1,4]{2,1,0:T(1,128)S(1)} all-gather(s32[1,1,4]{2,1,0:T(1,128)} %bitcast.146), channel_id=1, replica_groups=mesh['dp'=8,'shard'=4] {'shard'}, dimensions={0}, use_global_device_ids=true | all-gather | bytes 80 | tf_op jit(solution)/shard_map/all_gather | solution.py:101
  18.2 8.0 %all_gather.31 = s32[4,4,3]{2,1,0:T(4,128)S(1)} all-gather(s32[1,4,3]{2,1,0:T(4,128)S(1)} %copy.10), channel_id=1, replica_groups=mesh['dp'=8,'shard'=4] {'shard'}, dimensions={0}, use_global_device_ids=true | all-gather | bytes 240 | tf_op jit(solution)/shard_map/all_gather | solution.py:100
  26.2 7.2 %all-gather.4 = s32[4,1,512]{2,1,0:T(1,128)S(1)} all-gather(s32[1,1,512]{2,1,0:T(1,128)} %bitcast.144), channel_id=1, replica_groups=mesh['dp'=8,'shard'=4] {'shard'}, dimensions={0}, use_global_device_ids=true | all-gather | bytes 10240 | tf_op jit(solution)/shard_map/all_gather | solution.py:99
  33.6 14.3 %all-gather.10.cloned.1.call-done = f32[2048,256]{1,0:T(8,128)} async-done(((f32[512,256]{1,0:T(8,128)}), f32[2048,256]{1,0:T(8,128)}) %all-gather.10.cloned.1.call-update) | async-done | bytes 2097168 | tf_op jit(solution)/shard_map/all_gather | solution.py:98
  50.3 71.0 %while.103 = (s32[]{:T(128)}, f32[4,512]{1,0:T(4,128)S(1)}, f32[4,512]{1,0:T(4,128)S(1)}, f32[4,512]{1,0:T(4,128)S(1)}, pred[4,512]{1,0:T(4,128)(4,1)S(1)}, /*in...) while((s32[]{:T(128)}, f32[4,512]{1,0:T(4,128)S(1)}, ...), condition=%wide.region_6.7_spmd, body=%wide.region_0.6_spmd.sunk | while | flops 806631936 | bytes 6905463 | solution.py:111
  51.2 8.5 %gather_fusion = f32[512,256]{1,0:T(8,128)S(1)} fusion(f32[20480,256]{1,0:T(8,128)} %get-tuple-element.1221, s32[1024]{0:T(1024)S(1)} %pad_clamp_fusion.2), kind=kCustom, calls=%fused_computation.clone.1 | custom fusion | bytes 1050624 | tf_op jit(solution)/shard_map/while/body/eval_jaxpr/jit(_take)/gather | solution.py:29
  60.0 4.9 while.107
  66.8 8.5 %gather_fusion = f32[512,256]{1,0:T(8,128)S(1)} fusion(f32[20480,256]{1,0:T(8,128)} %get-tuple-element.1221, s32[1024]{0:T(1024)S(1)} %pad_clamp_fusion.2), kind=kCustom, calls=%fused_computation.clone.1 | custom fusion | bytes 1050624 | tf_op jit(solution)/shard_map/while/body/eval_jaxpr/jit(_take)/gather | solution.py:29
  75.6 9.1 %while.107 = (s32[]{:T(128)}, f32[512]{0:T(512)S(1)}, f32[512]{0:T(512)S(1)}, s32[]{:T(128)}, s32[3]{0:T(128)S(1)}, /*index=5*/f32[20480,256]{1,0:T(8,128)}, f32...) while((s32[]{:T(128)}, f32[512]{0:T(512)S(1)}, ...), condition=%wide.region_4.4_spmd, body=%wide.region_1.3_spmd.sunk | while | flops 806093824 | bytes 3172573 | solution.py:57
  86.7 8.5 %gather_fusion = f32[512,256]{1,0:T(8,128)S(1)} fusion(f32[20480,256]{1,0:T(8,128)} %get-tuple-element.1221, s32[1024]{0:T(1024)S(1)} %pad_clamp_fusion.2), kind=kCustom, calls=%fused_computation.clone.1 | custom fusion | bytes 1050624 | tf_op jit(solution)/shard_map/while/body/eval_jaxpr/jit(_take)/gather | solution.py:29
  95.5 4.9 while.107
  102.3 8.5 %gather_fusion = f32[512,256]{1,0:T(8,128)S(1)} fusion(f32[20480,256]{1,0:T(8,128)} %get-tuple-element.1221, s32[1024]{0:T(1024)S(1)} %pad_clamp_fusion.2), kind=kCustom, calls=%fused_computation.clone.1 | custom fusion | bytes 1050624 | tf_op jit(solution)/shard_map/while/body/eval_jaxpr/jit(_take)/gather | solution.py:29
  111.1 9.1 %while.107 = (s32[]{:T(128)}, f32[512]{0:T(512)S(1)}, f32[512]{0:T(512)S(1)}, s32[]{:T(128)}, s32[3]{0:T(128)S(1)}, /*index=5*/f32[20480,256]{1,0:T(8,128)}, f32...) while((s32[]{:T(128)}, f32[512]{0:T(512)S(1)}, ...), condition=%wide.region_4.4_spmd, body=%wide.region_1.3_spmd.sunk | while | flops 806093824 | bytes 3172573 | solution.py:57
  121.3 29.0 %all-gather.5 = f32[4,4,512]{2,1,0:T(4,128)S(1)} all-gather(f32[1,4,512]{2,1,0:T(4,128)S(1)} %bitcast.140), channel_id=2, replica_groups=mesh['dp'=8,'shard'=4] {'shard'}, dimensions={0}, use_global_device_ids=true | all-gather | bytes 40960 | tf_op jit(solution)/shard_map/all_gather | solution.py:13
  150.3 6.6 %all-gather.6 = f32[4,4,512]{2,1,0:T(4,128)S(1)} all-gather(f32[1,4,512]{2,1,0:T(4,128)S(1)} %bitcast.139), channel_id=3, replica_groups=mesh['dp'=8,'shard'=4] {'shard'}, dimensions={0}, use_global_device_ids=true | all-gather | bytes 40960 | tf_op jit(solution)/shard_map/all_gather | solution.py:13
  157.0 8.7 %all-gather.7 = f32[4,4,512]{2,1,0:T(4,128)S(1)} all-gather(f32[1,4,512]{2,1,0:T(4,128)S(1)} %bitcast.136), channel_id=4, replica_groups=mesh['dp'=8,'shard'=4] {'shard'}, dimensions={0}, use_global_device_ids=true | all-gather | bytes 40960 | tf_op jit(solution)/shard_map/all_gather | solution.py:13
  168.9 7.2 %broadcast_in_dim.94 = f32[20480,256]{1,0:T(8,128)} broadcast(f32[]{:T(128)} %constant.223.clone.1), dimensions={} | broadcast | bytes 20971524 | tf_op jit(solution)/shard_map/broadcast_in_dim | solution.py:118
  176.1 75.7 %while.106 = (s32[]{:T(128)}, f32[20480,256]{1,0:T(8,128)}, f32[4,512,256]{2,1,0:T(8,128)}, f32[4,512,256]{2,1,0:T(8,128)}, s32[4]{0:T(128)S(1)}, /*index=5*/s32...) while((s32[]{:T(128)}, f32[20480,256]{1,0:T(8,128)}, ...), condition=%wide.region_12.14_spmd, body=%wide.region_9.13_spmd.sunk | while | flops 2416838144 | bytes 11032662 | solution.py:126
  177.8 10.4 %while.108 = (s32[]{:T(128)}, f32[512,256]{1,0:T(8,128)S(1)}, f32[20480,256]{1,0:T(8,128)}, s32[]{:T(128)}, s32[3]{0:T(128)S(1)}, /*index=5*/f32[20480,256]{1,0:...) while((s32[]{:T(128)}, f32[512,256]{1,0:T(8,128)S(1)}, ...), condition=%wide.region_11.12_spmd, body=%wide.region_10.11_spmd.sunk | while | flops 2416443392 | bytes 7342317 | solution.py:80
  181.7 3.0 convolution_add_fusion.3
  184.7 2.9 fusion.47
  191.8 20.2 %while.108 = (s32[]{:T(128)}, f32[512,256]{1,0:T(8,128)S(1)}, f32[20480,256]{1,0:T(8,128)}, s32[]{:T(128)}, s32[3]{0:T(128)S(1)}, /*index=5*/f32[20480,256]{1,0:...) while((s32[]{:T(128)}, f32[512,256]{1,0:T(8,128)S(1)}, ...), condition=%wide.region_11.12_spmd, body=%wide.region_10.11_spmd.sunk | while | flops 2416443392 | bytes 7342317 | solution.py:80
  195.8 3.0 convolution_add_fusion.3
  205.5 3.0 convolution_add_fusion.3
  215.6 10.4 %while.108 = (s32[]{:T(128)}, f32[512,256]{1,0:T(8,128)S(1)}, f32[20480,256]{1,0:T(8,128)}, s32[]{:T(128)}, s32[3]{0:T(128)S(1)}, /*index=5*/f32[20480,256]{1,0:...) while((s32[]{:T(128)}, f32[512,256]{1,0:T(8,128)S(1)}, ...), condition=%wide.region_11.12_spmd, body=%wide.region_10.11_spmd.sunk | while | flops 2416443392 | bytes 7342317 | solution.py:80
  219.6 3.0 convolution_add_fusion.3
  229.7 20.2 %while.108 = (s32[]{:T(128)}, f32[512,256]{1,0:T(8,128)S(1)}, f32[20480,256]{1,0:T(8,128)}, s32[]{:T(128)}, s32[3]{0:T(128)S(1)}, /*index=5*/f32[20480,256]{1,0:...) while((s32[]{:T(128)}, f32[512,256]{1,0:T(8,128)S(1)}, ...), condition=%wide.region_11.12_spmd, body=%wide.region_10.11_spmd.sunk | while | flops 2416443392 | bytes 7342317 | solution.py:80
  233.6 3.0 convolution_add_fusion.3
  243.4 3.0 convolution_add_fusion.3
  253.5 25.4 %scatter_fusion = f32[20480,256]{1,0:T(8,128)} fusion(f32[20480,256]{1,0:T(8,128)} %get-tuple-element.581, s32[2048]{0:T(1024)S(1)} %bitcast.137, f32[2048,256]{1,0:T(8,128)S(1)} %bitcast.126), kind=kCustom, calls=%fused_computation.1 | custom fusion | flops 524288 | bytes 6299648 | tf_op jit(solution)/shard_map/scatter-add | solution.py:129
  279.5 52.4 %reduce-scatter.7.cloned.1.call-done = f32[1,512,256]{2,1,0:T(8,128)} async-done(((f32[4,512,256]{2,1,0:T(8,128)}), f32[1,512,256]{2,1,0:T(8,128)}) %reduce-scatter.7.cloned.1.call-update) | async-done | bytes 524304
  331.9 210.8 %reduce-scatter.5.cloned.1.call-done = f32[2560,256]{1,0:T(8,128)} async-done(((f32[20480,256]{1,0:T(8,128)}), f32[2560,256]{1,0:T(8,128)}) %reduce-scatter.5.cloned.1.call-update) | async-done | bytes 2621456 | tf_op jit(solution)/shard_map/reduce_scatter | solution.py:133
  (191 shorter events, 80.4 us)
Async XLA Ops:
  7.2 40.8 %all-gather.10.cloned.1.call-start = ((), (), s32[]{:S(2)}) async-start(), calls=%async_computation.2 | async-start | bytes 2621440 | tf_op jit(solution)/shard_map/all_gather | solution.py:98
  7.9 324.0 %reduce-scatter.7.cloned.1.call-start = ((), (), s32[]{:S(2)}) async-start(), calls=%async_computation.4 | async-start | bytes 2621440
  48.0 2.3 copy-start
  251.9 1.6 copy-start.1
  251.9 290.8 %reduce-scatter.5.cloned.1.call-start = ((), (), s32[]{:S(2)}) async-start(), calls=%async_computation.3 | async-start | bytes 23592960 | tf_op jit(solution)/shard_map/reduce_scatter | solution.py:133
Sparse Core Ops, SparseCore 0:
  9.8 38.0 all-gather.9
  252.0 79.8 reduce-scatter.6
  334.9 207.7 reduce-scatter.4
where the time goes:
time: 550 us; the launch traced here: 549 us
  waiting for transfers between devices  278 us (51%)
  blocking collectives  69 us (13%)
  local copies, waits for them, and re-layouts  62.3 us (11%)
  matrix products  60.1 us (11%)
  other arithmetic  44.5 us (8%)
  loops' own time  21.2 us (4%)
  between operations  13.8 us (3%)
    reduce_scatter x1, waiting for transfers between devices, local(): item_grad = lax.psum_scatter(d_local, 'dp', scatter_dimension=0, tiled=True)  211 us
    unnamed x4, waiting for transfers between devices  53.1 us
    all_gather x3, blocking collectives, joined(): gathered = jax.tree.map(lambda a: lax.all_gather(a, axis), part)  44.4 us
    gather x4, local copies, waits for them, and re-layouts, positive_row(): chosen = jnp.take(items, safe, axis=0)  34.1 us
    scatter-add x1, other arithmetic, local(): d_local.at[targets.reshape(-1)].add(updates.reshape(-1, width), mode='drop')  25.4 us
    dot_general x12, matrix products, tile_logits(): jnp.einsum('qd,td->qt', qblk, block, precision=lax.Precision.HIGHEST, pre...  25.2 us
    dot_general x6, matrix products, visit(): jnp.dot(prob, block, precision=high, preferred_element_type=jnp.float32)  17.8 us
    dot_general x6, matrix products, visit(): jnp.einsum('qt,qd->td', prob, qblk, precision=high, preferred_element_typ...  17.1 us
  transfers between devices with their start and end apart: 3, of which 3 were waited for; matrix products, arithmetic and copies ran while one was open for 5% of the time, Pallas kernels for 0%

commit v1 on v0

v1 whole, which is shorter than its diff:
```python
import functools

import jax
import jax.numpy as jnp
from jax import lax
from jax.experimental import pallas as pl
from jax.experimental.pallas import tpu as pltpu
from jax.sharding import PartitionSpec as P

TILE = 512
KMAX = 3
EXTRA = 8
MIB = 1024 * 1024

very_low = -1e30
high, highest = lax.Precision.HIGH, lax.Precision.HIGHEST


def dot(a, b, dims=((1,), (0,)), precision=high):
    return lax.dot_general(a, b, (dims, ((), ())), precision=precision, preferred_element_type=jnp.float32)


def pack_kernel(q_ref, row_ref, col_ref, lists_ref, out_ref):
    rows, width = q_ref.shape
    out_ref[:rows, :] = q_ref[...]
    out_ref[rows : rows + EXTRA, :] = jnp.zeros((EXTRA, width), jnp.float32)
    row, col = row_ref[...], col_ref[...]
    at_row = lax.broadcasted_iota(jnp.int32, (rows, rows), 1)
    at_col = lax.broadcasted_iota(jnp.int32, (rows, rows), 0)
    before = (row < col) | ((row == col) & (at_row < at_col))
    rank = jnp.sum(before.astype(jnp.float32), axis=1, keepdims=True)
    placed = rank == at_row.astype(jnp.float32)
    sorted_pos = jnp.sum(jnp.where(placed, col, 0.0), axis=0, keepdims=True)
    sorted_at = jnp.sum(jnp.where(placed, at_col.astype(jnp.float32), 0.0), axis=0, keepdims=True)
    per = rows // width
    for first, values in ((0, row), (per, sorted_pos), (2 * per, sorted_at)):
        for i in range(per):
            out_ref[rows + first + i : rows + first + i + 1, :] = values[:, i * width : (i + 1) * width]
    out_ref[rows + 3 * per : rows + 3 * per + 1, :] = lists_ref[...]


def pack(queries, positive, tile_ids, counts):
    rows, width = queries.shape
    lists = jnp.concatenate([tile_ids.reshape(-1), counts.reshape(-1)]).astype(jnp.float32)
    lists = jnp.pad(lists, (0, width - lists.shape[0])).reshape(1, width)
    pos = positive.astype(jnp.float32)
    return pl.pallas_call(
        pack_kernel,
        out_shape=jax.ShapeDtypeStruct((rows + EXTRA, width), jnp.float32),
        compiler_params=pltpu.CompilerParams(vmem_limit_bytes=24 * MIB),
        name="pack",
    )(queries, pos.reshape(1, rows), pos.reshape(rows, 1), lists)


def unpack(messages, shard_at, n_shard):
    rows, width = messages[0].shape[0] - EXTRA, messages[0].shape[1]
    per = rows // width
    meta = jnp.stack([m[rows:] for m in messages]).astype(jnp.int32)
    n = len(messages)
    pos = meta[:, :per].reshape(n, rows)
    sorted_pos = meta[:, per : 2 * per].reshape(n, rows)
    places = meta[:, 2 * per : 3 * per].reshape(n, rows)
    lists = meta[:, 3 * per]
    ids = lists[:, : n_shard * KMAX].reshape(n, n_shard, KMAX)
    cnt = lists[:, n_shard * KMAX : n_shard * (KMAX + 1)]
    ids = lax.dynamic_index_in_dim(ids, shard_at, 1, False)
    cnt = lax.dynamic_index_in_dim(cnt, shard_at, 1, False)
    return pos, sorted_pos, places, ids, cnt


def span(sorted_pos, start, length):
    return jnp.stack([jnp.sum(sorted_pos < start, axis=1), jnp.sum(sorted_pos < start + length, axis=1)], axis=1).astype(jnp.int32)


def swap(x, axis, bits):
    return lax.ppermute(x, axis, [(i, i ^ bits) for i in range(lax.axis_size(axis))])


def plane(message, half):
    n = lax.axis_size("shard")
    slots = [message]
    for j in range(1, n):
        top_bit, low_bit = 1 << (j.bit_length() - 1), j & -j
        if j == top_bit:
            slots.append(swap(message, "shard", j))
        else:
            first = swap(slots[j ^ top_bit][:half], "shard", top_bit)
            second = swap(slots[j ^ low_bit][half:], "shard", low_bit)
            slots.append((first, second))
            slots[j] = jnp.concatenate(slots[j], axis=0)
    return slots


def stats_kernel(n, base, ids, cnt, sorted_pos, places, where, *refs):
    msgs = refs[:n]
    pos_ref, items_hbm, acc_ref, chosen_ref, stat_ref, q_ref, tiles, items, rowbuf, sems = refs[n:]
    rows = q_ref.shape[1]
    local_rows = items.shape[0]
    for j in range(n):
        pltpu.make_async_copy(msgs[j].at[:rows], q_ref.at[j], sems.at[0, j]).start()

    def tile_copy(b, k):
        return pltpu.make_async_copy(
            items_hbm.at[pl.ds(pl.multiple_of(ids[b, k] * TILE, TILE), TILE)], tiles.at[b * KMAX + k], sems.at[1, b * KMAX + k]
        )

    for b in range(n):
        for k in range(KMAX):

            @pl.when(k < cnt[b])
            def _():
                tile_copy(b, k).start()

    whole = pltpu.make_async_copy(items_hbm, items, sems.at[2, 0])
    whole.start()
    for j in range(n):
        pltpu.make_async_copy(msgs[j].at[:rows], q_ref.at[j], sems.at[0, j]).wait()

    @pl.loop(0, n)
    def _(b):
        q_t = q_ref[b].T
        acc_ref[b] = jnp.zeros(acc_ref.shape[1:], jnp.float32)

        def visit(k, carry):
            top, total = carry
            tile_copy(b, k).wait()
            tile = tiles[b * KMAX + k]
            logits = dot(tile, q_t, precision=highest)
            new_top = jnp.maximum(top, jnp.max(logits, axis=0, keepdims=True))
            prob = jnp.exp(logits - new_top)
            scale = jnp.exp(top - new_top)
            total = total * scale + jnp.sum(prob, axis=0, keepdims=True)
            acc_ref[b] = acc_ref[b] * scale + dot(tile.T, prob)
            return new_top, total

        start = (jnp.full((1, rows), very_low, jnp.float32), jnp.zeros((1, rows), jnp.float32))
        top, total = lax.fori_loop(0, cnt[b], visit, start)
        stat_ref[b, 0:1, :] = top
        stat_ref[b, 1:2, :] = total

    whole.wait()

    @pl.loop(0, n)
    def _(b):
        rowbuf[...] = jnp.zeros(rowbuf.shape, jnp.float32)

        @pl.loop(where[b, 0], where[b, 1])
        def _(i):
            rowbuf[pl.ds(places[b, i], 1), :] = items[pl.ds(sorted_pos[b, i] - base[0], 1), :]

        chosen = rowbuf[...].T
        chosen_ref[b] = chosen
        offset = pos_ref[pl.ds(b, 1), :] - base[0]
        inside = (offset >= 0) & (offset < local_rows)
        plogit = jnp.sum(q_ref[b].T * chosen, axis=0, keepdims=True)
        top, total = stat_ref[b, 0:1, :], stat_ref[b, 1:2, :]
        new_top = jnp.maximum(top, jnp.where(inside, plogit, very_low))
        total = total * jnp.exp(top - new_top) + jnp.where(inside, jnp.exp(plogit - new_top), 0.0)
        stat_ref[b, 1:2, :] = new_top + jnp.log(total)
        stat_ref[b, 2:3, :] = jnp.where(inside, plogit, 0.0)
        stat_ref[b, 3:4, :] = jnp.where(inside, 1.0, 0.0)
        stat_ref[b, 4:8, :] = jnp.zeros((4, rows), jnp.float32)


def stats(messages, meta, items, base):
    n = len(messages)
    rows, width = messages[0].shape[0] - EXTRA, messages[0].shape[1]
    pos, sorted_pos, places, ids, cnt = meta
    smem, hbm = pl.BlockSpec(memory_space=pltpu.SMEM), pl.BlockSpec(memory_space=pl.ANY)
    vmem = pl.BlockSpec(memory_space=pltpu.VMEM)
    return pl.pallas_call(
        functools.partial(stats_kernel, n),
        out_shape=(
            jax.ShapeDtypeStruct((n, width, rows), jnp.float32),
            jax.ShapeDtypeStruct((n, width, rows), jnp.float32),
            jax.ShapeDtypeStruct((n, 8, rows), jnp.float32),
        ),
        in_specs=[smem] * 6 + [hbm] * n + [vmem, hbm],
        out_specs=(vmem, vmem, vmem),
        scratch_shapes=[
            pltpu.VMEM((n, rows, width), jnp.float32),
            pltpu.VMEM((n * KMAX, TILE, width), jnp.float32),
            pltpu.VMEM(items.shape, jnp.float32),
            pltpu.VMEM((rows, width), jnp.float32),
            pltpu.SemaphoreType.DMA((3, n * KMAX)),
        ],
        compiler_params=pltpu.CompilerParams(vmem_limit_bytes=56 * MIB),
        name="stats",
    )(base, ids, cnt, sorted_pos, places, span(sorted_pos, base[0], items.shape[0]), *messages, pos, items)


def dq_kernel(acc_ref, chosen_ref, stat_ref, lse_ref, plog_ref, first_ref, second_ref):
    n, _, rows = acc_ref.shape
    half = rows // 2

    @pl.loop(0, n)
    def _(b):
        lse = lse_ref[pl.ds(b, 1), :]
        weight = (jnp.exp(plog_ref[pl.ds(b, 1), :] - lse) - 1.0) * stat_ref[b, 3:4, :]
        d = (acc_ref[b] * jnp.exp(stat_ref[b, 0:1, :] - lse) + chosen_ref[b] * weight).T
        first_ref[b] = d[:half]
        second_ref[b] = d[half:]


def dq_shares(acc, chosen, stat, lse, plog):
    n, width, rows = acc.shape
    out = jax.ShapeDtypeStruct((n, rows // 2, width), jnp.float32)
    return pl.pallas_call(
        dq_kernel, out_shape=(out, out), compiler_params=pltpu.CompilerParams(vmem_limit_bytes=32 * MIB), name="dq"
    )(acc, chosen, stat, lse, plog)


def reduce_slots(shares, order):
    slots = {j: shares[j] for j in range(shares.shape[0])}
    for bit in order:
        out = [j for j in sorted(slots) if j & bit]
        got = swap(jnp.stack([slots[j] for j in out]), "shard", bit)
        slots = {j ^ bit: slots[j ^ bit] + got[i] for i, j in enumerate(out)}
    return slots[0]


def item_kernel(n, base, ids, cnt, sorted_pos, places, where, weight, *refs):
    msgs = refs[:n]
    lse_ref, items_hbm, acc_hbm, out_hbm, q_ref, items, acc, sems = refs[n:]
    rows = q_ref.shape[1]
    span_rows = acc.shape[0]
    tiles = span_rows // TILE
    get_acc = pltpu.make_async_copy(acc_hbm, acc, sems.at[n])
    get_acc.start()
    get_items = pltpu.make_async_copy(
        items_hbm.at[pl.ds(pl.multiple_of(base[1] * TILE, TILE), span_rows)], items, sems.at[n + 1]
    )
    get_items.start()
    for j in range(n):
        pltpu.make_async_copy(msgs[j].at[:rows], q_ref.at[j], sems.at[j]).start()
    get_acc.wait()
    get_items.wait()
    for j in range(n):
        pltpu.make_async_copy(msgs[j].at[:rows], q_ref.at[j], sems.at[j]).wait()

    @pl.loop(0, n)
    def _(b):
        @pl.loop(0, cnt[b])
        def _(k):
            tile = ids[b, k] - base[1]

            @pl.when((tile >= 0) & (tile < tiles))
            def _():
                at = pl.ds(pl.multiple_of(tile * TILE, TILE), TILE)
                q = q_ref[b]
                logits = dot(items[at, :], q, ((1,), (1,)), highest)
                prob = jnp.exp(logits - lse_ref[pl.ds(b, 1), :])
                acc[at, :] += dot(prob, q)

        @pl.loop(where[b, 0], where[b, 1])
        def _(i):
            place = places[b, i]
            at = pl.ds(sorted_pos[b, i] - base[0], 1)
            acc[at, :] += q_ref[b, pl.ds(place, 1), :] * weight[b, place]

    put = pltpu.make_async_copy(acc, out_hbm, sems.at[n])
    put.start()
    put.wait()


def item_grads(messages, meta, lse, weight, items, acc, base):
    n = len(messages)
    rows, width = messages[0].shape[0] - EXTRA, messages[0].shape[1]
    _, sorted_pos, places, ids, cnt = meta
    smem, hbm = pl.BlockSpec(memory_space=pltpu.SMEM), pl.BlockSpec(memory_space=pl.ANY)
    vmem = pl.BlockSpec(memory_space=pltpu.VMEM)
    return pl.pallas_call(
        functools.partial(item_kernel, n),
        out_shape=jax.ShapeDtypeStruct(acc.shape, jnp.float32),
        in_specs=[smem] * 7 + [hbm] * n + [vmem, hbm, hbm],
        out_specs=hbm,
        scratch_shapes=[
            pltpu.VMEM((n, rows, width), jnp.float32),
            pltpu.VMEM(acc.shape, jnp.float32),
            pltpu.VMEM(acc.shape, jnp.float32),
            pltpu.SemaphoreType.DMA((n + 2,)),
        ],
        input_output_aliases={7 + n + 2: 0},
        compiler_params=pltpu.CompilerParams(vmem_limit_bytes=32 * MIB),
        name="item_grads",
    )(base, ids, cnt, sorted_pos, places, span(sorted_pos, base[0], acc.shape[0]), weight, *messages, lse, items, acc)


def local(queries, items, positive, tile_ids, counts):
    dp_at, shard_at = lax.axis_index("dp"), lax.axis_index("shard")
    n_dp, n_shard = lax.axis_size("dp"), lax.axis_size("shard")
    rows, width = queries.shape
    local_rows = items.shape[0]
    own_rows = local_rows // n_dp
    half = rows // 2

    message = pack(queries, positive, tile_ids, counts)
    far = [message] + [swap(message, "dp", 2 * k) for k in range(1, n_dp // 2)]
    group = plane(message, half)
    groups = [group] + [plane(m, half) for m in far[1:]]
    metas = [unpack(g, shard_at, n_shard) for g in groups]

    item_base = (shard_at * local_rows).astype(jnp.int32)
    acc, chosen, stat = stats(group, metas[0], items, item_base.reshape(1))

    parts = stat[:, 1:3]
    bit = 1
    while bit < n_shard:
        got = swap(parts, "shard", bit)
        got = got[jnp.array([j ^ bit for j in range(n_shard)])]
        top = jnp.maximum(parts[:, 0], got[:, 0])
        lse = top + jnp.log(jnp.exp(parts[:, 0] - top) + jnp.exp(got[:, 0] - top))
        parts = jnp.stack([lse, parts[:, 1] + got[:, 1]], axis=1)
        bit *= 2
    lse, plog = parts[:, 0], parts[:, 1]
    loss = lse[0] - plog[0]

    first, second = dq_shares(acc, chosen, stat, lse, plog)
    bits = [1 << i for i in range(n_shard.bit_length() - 1)]
    query_grad = jnp.concatenate([reduce_slots(first, bits), reduce_slots(second, bits[::-1])], axis=0)

    pair_rows = 2 * own_rows
    pair_at = dp_at // 2
    base = jnp.stack([item_base + pair_at * pair_rows, pair_at * pair_rows // TILE]).astype(jnp.int32)
    weight = jnp.exp(plog - lse) - 1.0
    sent = jnp.stack([lse, weight], axis=1)
    terms = [sent] + [swap(sent, "dp", 2 * k) for k in range(1, n_dp // 2)]
    grads = jnp.zeros((pair_rows, width), jnp.float32)
    for g, meta, term in zip(groups, metas, terms):
        grads = item_grads(g, meta, term[:, 0], term[:, 1], items, grads, base)
    core = dp_at % 2
    mine = lax.dynamic_slice_in_dim(grads, core * own_rows, own_rows, 0)
    other = lax.dynamic_slice_in_dim(grads, (1 - core) * own_rows, own_rows, 0)
    item_grad = mine + swap(other, "dp", 1)
    return loss, query_grad, item_grad


def solution(mesh):
    placed = (
        P(("dp", "shard"), None),
        P("shard", None),
        P(("dp", "shard")),
        P(("dp", "shard"), None, None),
        P(("dp", "shard"), None),
    )
    return jax.shard_map(
        local,
        mesh=mesh,
        in_specs=placed,
        out_specs=(P(("dp", "shard")), P(("dp", "shard"), None), P(("shard", "dp"), None)),
        check_vma=False,
    )
```

time: 550 us -> 245 us (0.45)
  waiting for transfers between devices: 278 us -> 56.5 us
  blocking collectives: 69 us -> 0 us
  Pallas kernels: 0 us -> 64.2 us
  matrix products: 60.1 us -> 0 us
  starting transfers between devices: 0.12 us -> 46.9 us
  loops' own time: 21.2 us -> 0 us
  other arithmetic: 44.5 us -> 25.5 us
  local copies, waits for them, and re-layouts: 62.3 us -> 46.8 us
  between operations: 13.8 us -> 1.14 us
    reduce_scatter x1 -> x0, waiting for transfers between devices: 211 us -> none  [local(): item_grad = lax.psum_scatter(d_local, 'dp', scatter_dimension=0, tiled=True)]
    all_gather x6 -> x0, blocking collectives: 69 us -> none  [the longest x3 44.4 us: joined(): gathered = jax.tree.map(lambda a: lax.all_gather(a, axis), part)]
    pallas_call x0 -> x7, Pallas kernels: none -> 64.2 us  [the longest x4 35.3 us: item_grads(): pl.pallas_call(functools.partial(item_kernel, n), out_shape=jax.ShapeDtyp...]
    dot_general x24 -> x0, matrix products: 60.1 us -> none  [the longest x12 25.2 us: tile_logits(): jnp.einsum('qd,td->qt', qblk, block, precision=lax.Precision.HIGHEST, pre...]
    ppermute x0 -> x29, waiting for transfers between devices: none -> 56.5 us  [swap(): lax.ppermute(x, axis, [(i, i ^ bits) for i in range(lax.axis_size(axis))])]
    unnamed x4 -> x0, waiting for transfers between devices: 53.1 us -> none
    ppermute x0 -> x29, starting transfers between devices: none -> 46.9 us  [swap(): lax.ppermute(x, axis, [(i, i ^ bits) for i in range(lax.axis_size(axis))])]
    gather x4 -> x2, local copies, waits for them, and re-layouts: 34.1 us -> 1.15 us  [local(): got = got[jnp.array([j ^ bit for j in range(n_shard)])]]
  transfers between devices with their start and end apart: 3 -> 29, of which waited for: 3 -> 16; matrix products, arithmetic and copies ran while one was open for 5% -> 20% of each run, Pallas kernels for 0% -> 16%
where the time goes in v1:
time: 245 us; the launch traced here: 241 us
  Pallas kernels  64.2 us (26%)
  waiting for transfers between devices  56.5 us (23%)
  starting transfers between devices  46.9 us (19%)
  local copies, waits for them, and re-layouts  46.8 us (19%)
  other arithmetic  25.5 us (10%)
    ppermute x29, waiting for transfers between devices, swap(): lax.ppermute(x, axis, [(i, i ^ bits) for i in range(lax.axis_size(axis))])  56.5 us
    ppermute x29, starting transfers between devices, swap(): lax.ppermute(x, axis, [(i, i ^ bits) for i in range(lax.axis_size(axis))])  46.9 us
    pallas_call x4, Pallas kernels, item_grads(): pl.pallas_call(functools.partial(item_kernel, n), out_shape=jax.ShapeDtyp...  35.3 us
    pallas_call x1, Pallas kernels, stats(): pl.pallas_call(functools.partial(stats_kernel, n), out_shape=(jax.ShapeDt...  27.6 us
    unnamed x65, local copies, waits for them, and re-layouts  21.7 us
    another operation x10, local copies, waits for them, and re-layouts, span(): jnp.stack([jnp.sum(sorted_pos < start, axis=1), jnp.sum(sorted_pos < star...  8.03 us
    unnamed x8, other arithmetic  5.02 us
  transfers between devices with their start and end apart: 29, of which 16 were waited for; matrix products, arithmetic and copies ran while one was open for 20% of the time, Pallas kernels for 16%

profile of v1, /device:TPU:0, one launch (start us, length us, event | category | flops | bytes accessed | tf_op | source)
XLA Modules:
  0.0 241.1 jit_solution(7759629997885053314)
XLA Ops:
  4.6 3.0 %collective-permute-start.1 = (f32[520,256]{1,0:T(8,128)S(1)}, f32[520,256]{1,0:T(8,128)S(1)}, u32[]{:S(2)}, u32[]{:S(2)}) collective-permute-start(f32[520,256]{1,0:T(8,128)S(1)} %pack.1.refs_0_), channel_id=1, source_target_pairs={{0,2},{1,3},{2,0},{3,1},{4,6},{5,7},{6,4},{7,5},{8,10},{9,11},{10,... | collective-permute-start | bytes 1597448 | tf_op jit(solution)/shard_map/ppermute | solution.py:76
  10.7 2.6 %collective-permute-start.16 = (f32[520,256]{1,0:T(8,128)S(1)}, f32[520,256]{1,0:T(8,128)}, u32[]{:S(2)}, u32[]{:S(2)}) collective-permute-start(f32[520,256]{1,0:T(8,128)S(1)} %pack.1.refs_0_), channel_id=1, source_target_pairs={{0,16},{4,20},{8,24},{12,28},{16,0},{20,4},{24,8},{28,12},{1,17},{... | collective-permute-start | bytes 1597448 | tf_op jit(solution)/shard_map/ppermute | solution.py:76
  14.9 4.8 %collective-permute-done.1.refs_2_ = f32[520,256]{1,0:T(8,128)S(1)} collective-permute-done((f32[520,256]{1,0:T(8,128)S(1)}, f32[520,256]{1,0:T(8,128)S(1)}, u32[]{:S(2)}, u32[]{:S(2)}) %collective-permute-start.1) | collective-permute-done | bytes 532512 | tf_op jit(solution)/shard_map/ppermute | solution.py:76
  19.8 1.8 collective-permute-start.2
  21.6 1.6 collective-permute-start.3
  23.2 9.7 %collective-permute-done.22.refs_0_ = f32[520,256]{1,0:T(8,128)} collective-permute-done((f32[520,256]{1,0:T(8,128)S(1)}, f32[520,256]{1,0:T(8,128)}, u32[]{:S(2)}, u32[]{:S(2)}) %collective-permute-start.22) | collective-permute-done | bytes 532512 | tf_op jit(solution)/shard_map/ppermute | solution.py:76
  34.7 14.9 %collective-permute-done.16.refs_0_ = f32[520,256]{1,0:T(8,128)} collective-permute-done((f32[520,256]{1,0:T(8,128)S(1)}, f32[520,256]{1,0:T(8,128)}, u32[]{:S(2)}, u32[]{:S(2)}) %collective-permute-start.16) | collective-permute-done | bytes 532512 | tf_op jit(solution)/shard_map/ppermute | solution.py:76
  56.1 27.6 %stats.1 = (f32[4,256,512]{2,1,0:T(8,128)}, f32[4,256,512]{2,1,0:T(8,128)}, f32[4,8,512]{2,1,0:T(8,128)}) custom-call(s32[1]{0:T(128)} %bitcast.base, s32[4,3]{1,0:T(4,128)} %bitcast.173, s32[4]{0:T(128)} %fusion.36.cnt, s32[4,512]{1,0:T(4,128)} %bitcast.161, s32[4,512]{1,0:T(4,128)} %bitcast.163, s32[4,2]{1,0:T(4,128)} %pad_add_fusion.where, ...), custom_call_target="tpu_custom_call" | custom-call | tf_op jit(solution)/shard_map/stats/pallas_call | solution.py:171
  84.5 5.5 %collective-permute-start.4 = (f32[4,2,512]{2,1,0:T(2,128)S(1)}, f32[4,2,512]{2,1,0:T(2,128)S(1)}, u32[]{:S(2)}, u32[]{:S(2)}) collective-permute-start(f32[4,2,512]{2,1,0:T(2,128)S(1)} %slice.234), channel_id=1, source_target_pairs={{0,1},{1,0},{2,3},{3,2},{4,5},{5,4},{6,7},{7,6},{8,9},{9,8},{10,11... | collective-permute-start | bytes 49160 | tf_op jit(solution)/shard_map/ppermute | solution.py:76
  91.7 2.0 collective-permute-start.17
  95.9 2.2 collective-permute-done.5
  101.6 9.9 %item_grads.4.refs_6_ = f32[5120,256]{1,0:T(8,128)S(1)} custom-call(s32[2]{0:T(128)S(1)} %pad_add_fusion.5.base, s32[4,3]{1,0:T(4,128)S(1)} %bitcast.174, s32[4]{0:T(128)S(1)} %copy-done.18, s32[4,512]{1,0:T(4,128)S(1)} %bitcast.162, s32[4,512]{1,0:T(4,128)S(1)} %bitcast.164, s32[4,2]{1,0:T(4,128)S(1)} %pad_add_fusion.4.where, ...), custom_call_target="tpu_custom_call", output_to_operand_aliasing={{}: (13, {})} | custom-call | tf_op jit(solution)/shard_map/item_grads/pallas_call | solution.py:272
  111.5 2.3 copy-done
  115.1 3.4 %collective-permute-done.20 = f32[4,2,512]{2,0,1:T(4,128)S(1)} collective-permute-done((f32[4,2,512]{2,0,1:T(4,128)S(1)}, f32[4,2,512]{2,0,1:T(4,128)S(1)}, u32[]{:S(2)}, u32[]{:S(2)}) %collective-permute-start.20) | collective-permute-done | bytes 16416 | tf_op jit(solution)/shard_map/ppermute | solution.py:76
  118.5 2.5 %collective-permute-start.14 = (f32[4,2,512]{2,0,1:T(4,128)S(1)}, f32[4,2,512]{2,0,1:T(4,128)S(1)}, u32[]{:S(2)}, u32[]{:S(2)}) collective-permute-start(f32[4,2,512]{2,0,1:T(4,128)S(1)} %pad_maximum_fusion.6), channel_id=1, source_target_pairs={{0,24},{4,28},{8,16},{12,20},{16,8},{20,12},{24,0},{28,4},{1,25},{... | collective-permute-start | bytes 49160 | tf_op jit(solution)/shard_map/ppermute | solution.py:76
  121.0 3.0 %collective-permute-done.14 = f32[4,2,512]{2,0,1:T(4,128)S(1)} collective-permute-done((f32[4,2,512]{2,0,1:T(4,128)S(1)}, f32[4,2,512]{2,0,1:T(4,128)S(1)}, u32[]{:S(2)}, u32[]{:S(2)}) %collective-permute-start.14) | collective-permute-done | bytes 16416 | tf_op jit(solution)/shard_map/ppermute | solution.py:76
  124.0 4.3 %collective-permute-start.11 = (f32[520,256]{1,0:T(8,128)}, f32[520,256]{1,0:T(8,128)S(1)}, u32[]{:S(2)}, u32[]{:S(2)}) collective-permute-start(f32[520,256]{1,0:T(8,128)} %collective-permute-done.10.refs_0_), channel_id=1, source_target_pairs={{0,1},{1,0},{2,3},{3,2},{4,5},{5,4},{6,7},{7,6},{8,9},{9,8},{10,11... | collective-permute-start | bytes 1597448 | tf_op jit(solution)/shard_map/ppermute | solution.py:76
  130.4 2.1 collective-permute-start.19
  133.5 1.6 collective-permute-start.21
  135.9 2.1 collective-permute-start.13
  174.2 2.5 %copy-done.1 = f32[5120,256]{1,0:T(8,128)S(1)} copy-done((f32[5120,256]{1,0:T(8,128)S(1)}, f32[5120,256]{1,0:T(8,128)}, u32[]{:S(2)}) %copy-start.1) | copy-done | bytes 5242904
  176.7 6.6 %item_grads.5.refs_6_ = f32[5120,256]{1,0:T(8,128)S(1)} custom-call(s32[2]{0:T(128)S(1)} %pad_add_fusion.5.base, s32[4,3]{1,0:T(4,128)S(1)} %bitcast.177, s32[4]{0:T(128)S(1)} %fusion.39.cnt, s32[4,512]{1,0:T(4,128)S(1)} %bitcast.169, s32[4,512]{1,0:T(4,128)S(1)} %bitcast.170, s32[4,2]{1,0:T(4,128)S(1)} %pad_add_fusion.3.where, ...), custom_call_target="tpu_custom_call", output_to_operand_aliasing={{}: (13, {})} | custom-call | tf_op jit(solution)/shard_map/item_grads/pallas_call | solution.py:272
  183.3 8.6 %item_grads.6.refs_6_ = f32[5120,256]{1,0:T(8,128)S(1)} custom-call(s32[2]{0:T(128)S(1)} %pad_add_fusion.5.base, s32[4,3]{1,0:T(4,128)S(1)} %bitcast.176, s32[4]{0:T(128)S(1)} %fusion.38.cnt, s32[4,512]{1,0:T(4,128)S(1)} %bitcast.167, s32[4,512]{1,0:T(4,128)S(1)} %bitcast.168, s32[4,2]{1,0:T(4,128)S(1)} %pad_add_fusion.2.where, ...), custom_call_target="tpu_custom_call", output_to_operand_aliasing={{}: (13, {})} | custom-call | tf_op jit(solution)/shard_map/item_grads/pallas_call | solution.py:272
  191.9 10.2 %item_grads.7 = f32[5120,256]{1,0:T(8,128)S(1)} custom-call(s32[2]{0:T(128)S(1)} %pad_add_fusion.5.base, s32[4,3]{1,0:T(4,128)S(1)} %bitcast.175, s32[4]{0:T(128)S(1)} %fusion.37.cnt, s32[4,512]{1,0:T(4,128)S(1)} %bitcast.165, s32[4,512]{1,0:T(4,128)S(1)} %bitcast.166, s32[4,2]{1,0:T(4,128)S(1)} %pad_add_fusion.1.where, ...), custom_call_target="tpu_custom_call", output_to_operand_aliasing={{}: (13, {})} | custom-call | tf_op jit(solution)/shard_map/item_grads/pallas_call | solution.py:272
  202.1 1.7 constant_dynamic-slice_fusion.6
  203.8 2.2 copy-done.2
  208.9 5.4 %collective-permute-start.6 = (f32[2,256,256]{2,1,0:T(8,128)}, f32[2,256,256]{2,1,0:T(8,128)S(1)}, u32[]{:S(2)}, u32[]{:S(2)}) collective-permute-start(f32[2,256,256]{2,1,0:T(8,128)} %pad_maximum_fusion.3), channel_id=1, source_target_pairs={{0,1},{1,0},{2,3},{3,2},{4,5},{5,4},{6,7},{7,6},{8,9},{9,8},{10,11... | collective-permute-start | bytes 1572872 | tf_op jit(solution)/shard_map/ppermute | solution.py:76
  215.1 2.1 collective-permute-start.8
  217.2 8.8 %collective-permute-done.6 = f32[2,256,256]{2,1,0:T(8,128)S(1)} collective-permute-done((f32[2,256,256]{2,1,0:T(8,128)}, f32[2,256,256]{2,1,0:T(8,128)S(1)}, u32[]{:S(2)}, u32[]{:S(2)}) %collective-permute-start.6) | collective-permute-done | bytes 524320 | tf_op jit(solution)/shard_map/ppermute | solution.py:76
  226.0 2.1 collective-permute-start.7
  230.6 3.6 %collective-permute-done.7 = f32[1,256,256]{2,1,0:T(8,128)S(1)} collective-permute-done((f32[1,256,256]{2,1,0:T(8,128)S(1)}, f32[1,256,256]{2,1,0:T(8,128)S(1)}, u32[]{:S(2)}, u32[]{:S(2)}) %collective-permute-start.7) | collective-permute-done | bytes 262176 | tf_op jit(solution)/shard_map/ppermute | solution.py:76
  236.7 4.4 %dynamic-slice_add_fusion = f32[2560,256]{1,0:T(8,128)} fusion(f32[2560,256]{1,0:T(8,128)} %collective-permute-done.28, f32[5120,256]{1,0:T(8,128)} %copy-done.2, s32[]{:T(128)S(6)} %select_n.44), kind=kLoop, calls=%fused_computation.2 | loop fusion | flops 655360 | bytes 7864324 | tf_op jit(solution)/shard_map/add | solution.py:334
  (212 shorter events, 74.7 us)
Async XLA Ops:
  4.6 50.6 %copy-start.3 = (f32[520,256]{1,0:T(8,128)}, f32[520,256]{1,0:T(8,128)S(1)}, u32[]{:S(2)}) copy-start(f32[520,256]{1,0:T(8,128)S(1)} %pack.1.refs_0_) | copy-start | bytes 1597444
  4.6 15.1 %collective-permute-start.1 = (f32[520,256]{1,0:T(8,128)S(1)}, f32[520,256]{1,0:T(8,128)S(1)}, u32[]{:S(2)}, u32[]{:S(2)}) collective-permute-start(f32[520,256]{1,0:T(8,128)S(1)} %pack.1.refs_0_), channel_id=1, source_target_pairs={{0,2},{1,3},{2,0},{3,1},{4,6},{5,7},{6,4},{7,5},{8,10},{9,11},{10,... | collective-permute-start | bytes 1597448 | tf_op jit(solution)/shard_map/ppermute | solution.py:76
  7.7 13.9 %collective-permute-start = (f32[520,256]{1,0:T(8,128)S(1)}, f32[520,256]{1,0:T(8,128)S(1)}, u32[]{:S(2)}, u32[]{:S(2)}) collective-permute-start(f32[520,256]{1,0:T(8,128)S(1)} %pack.1.refs_0_), channel_id=1, source_target_pairs={{0,1},{1,0},{2,3},{3,2},{4,5},{5,4},{6,7},{7,6},{8,9},{9,8},{10,11... | collective-permute-start | bytes 1597448 | tf_op jit(solution)/shard_map/ppermute | solution.py:76
  9.1 23.7 %collective-permute-start.22 = (f32[520,256]{1,0:T(8,128)S(1)}, f32[520,256]{1,0:T(8,128)}, u32[]{:S(2)}, u32[]{:S(2)}) collective-permute-start(f32[520,256]{1,0:T(8,128)S(1)} %pack.1.refs_0_), channel_id=1, source_target_pairs={{0,8},{4,12},{8,0},{12,4},{16,24},{20,28},{24,16},{28,20},{1,9},{5... | collective-permute-start | bytes 1597448 | tf_op jit(solution)/shard_map/ppermute | solution.py:76
  10.7 38.9 %collective-permute-start.16 = (f32[520,256]{1,0:T(8,128)S(1)}, f32[520,256]{1,0:T(8,128)}, u32[]{:S(2)}, u32[]{:S(2)}) collective-permute-start(f32[520,256]{1,0:T(8,128)S(1)} %pack.1.refs_0_), channel_id=1, source_target_pairs={{0,16},{4,20},{8,24},{12,28},{16,0},{20,4},{24,8},{28,12},{1,17},{... | collective-permute-start | bytes 1597448 | tf_op jit(solution)/shard_map/ppermute | solution.py:76
  13.3 81.1 %collective-permute-start.10 = (f32[520,256]{1,0:T(8,128)S(1)}, f32[520,256]{1,0:T(8,128)}, u32[]{:S(2)}, u32[]{:S(2)}) collective-permute-start(f32[520,256]{1,0:T(8,128)S(1)} %pack.1.refs_0_), channel_id=1, source_target_pairs={{0,24},{4,28},{8,16},{12,20},{16,8},{20,12},{24,0},{28,4},{1,25},{... | collective-permute-start | bytes 1597448 | tf_op jit(solution)/shard_map/ppermute | solution.py:76
  19.8 35.5 %copy-start.5 = (f32[520,256]{1,0:T(8,128)}, f32[520,256]{1,0:T(8,128)S(1)}, u32[]{:S(2)}) copy-start(f32[520,256]{1,0:T(8,128)S(1)} %collective-permute-done.1.refs_2_) | copy-start | bytes 1597444
  19.8 30.9 %collective-permute-start.2 = (f32[264,256]{1,0:T(8,128)S(1)}, f32[264,256]{1,0:T(8,128)S(1)}, u32[]{:S(2)}, u32[]{:S(2)}) collective-permute-start(f32[264,256]{1,0:T(8,128)S(1)} %slice.299), channel_id=1, source_target_pairs={{0,1},{1,0},{2,3},{3,2},{4,5},{5,4},{6,7},{7,6},{8,9},{9,8},{10,11... | collective-permute-start | bytes 811016 | tf_op jit(solution)/shard_map/ppermute | solution.py:76
  21.6 33.7 %copy-start.7 = (f32[520,256]{1,0:T(8,128)}, f32[520,256]{1,0:T(8,128)S(1)}, u32[]{:S(2)}) copy-start(f32[520,256]{1,0:T(8,128)S(1)} %collective-permute-done.refs_1_) | copy-start | bytes 1597444
  21.6 28.5 %collective-permute-start.3 = (f32[256,256]{1,0:T(8,128)S(1)}, f32[256,256]{1,0:T(8,128)S(1)}, u32[]{:S(2)}, u32[]{:S(2)}) collective-permute-start(f32[256,256]{1,0:T(8,128)S(1)} %slice.303), channel_id=1, source_target_pairs={{0,2},{1,3},{2,0},{3,1},{4,6},{5,7},{6,4},{7,5},{8,10},{9,11},{10,... | collective-permute-start | bytes 786440 | tf_op jit(solution)/shard_map/ppermute | solution.py:76
  32.9 91.1 %collective-permute-start.24 = (f32[520,256]{1,0:T(8,128)}, f32[520,256]{1,0:T(8,128)S(1)}, u32[]{:S(2)}, u32[]{:S(2)}) collective-permute-start(f32[520,256]{1,0:T(8,128)} %collective-permute-done.22.refs_0_), channel_id=1, source_target_pairs={{0,2},{1,3},{2,0},{3,1},{4,6},{5,7},{6,4},{7,5},{8,10},{9,11},{10,... | collective-permute-start | bytes 1597448 | tf_op jit(solution)/shard_map/ppermute | solution.py:76
  49.6 78.8 %collective-permute-start.23 = (f32[520,256]{1,0:T(8,128)}, f32[520,256]{1,0:T(8,128)}, u32[]{:S(2)}, u32[]{:S(2)}) collective-permute-start(f32[520,256]{1,0:T(8,128)} %collective-permute-done.22.refs_0_), channel_id=1, source_target_pairs={{0,1},{1,0},{2,3},{3,2},{4,5},{5,4},{6,7},{7,6},{8,9},{9,8},{10,11... | collective-permute-start | bytes 1597448 | tf_op jit(solution)/shard_map/ppermute | solution.py:76
  50.1 80.0 %collective-permute-start.18 = (f32[520,256]{1,0:T(8,128)}, f32[520,256]{1,0:T(8,128)S(1)}, u32[]{:S(2)}, u32[]{:S(2)}) collective-permute-start(f32[520,256]{1,0:T(8,128)} %collective-permute-done.16.refs_0_), channel_id=1, source_target_pairs={{0,2},{1,3},{2,0},{3,1},{4,6},{5,7},{6,4},{7,5},{8,10},{9,11},{10,... | collective-permute-start | bytes 1597448 | tf_op jit(solution)/shard_map/ppermute | solution.py:76
  84.5 7.2 %collective-permute-start.4 = (f32[4,2,512]{2,1,0:T(2,128)S(1)}, f32[4,2,512]{2,1,0:T(2,128)S(1)}, u32[]{:S(2)}, u32[]{:S(2)}) collective-permute-start(f32[4,2,512]{2,1,0:T(2,128)S(1)} %slice.234), channel_id=1, source_target_pairs={{0,1},{1,0},{2,3},{3,2},{4,5},{5,4},{6,7},{7,6},{8,9},{9,8},{10,11... | collective-permute-start | bytes 49160 | tf_op jit(solution)/shard_map/ppermute | solution.py:76
  91.7 38.7 %collective-permute-start.17 = (f32[520,256]{1,0:T(8,128)}, f32[520,256]{1,0:T(8,128)S(1)}, u32[]{:S(2)}, u32[]{:S(2)}) collective-permute-start(f32[520,256]{1,0:T(8,128)} %collective-permute-done.16.refs_0_), channel_id=1, source_target_pairs={{0,1},{1,0},{2,3},{3,2},{4,5},{5,4},{6,7},{7,6},{8,9},{9,8},{10,11... | collective-permute-start | bytes 1597448 | tf_op jit(solution)/shard_map/ppermute | solution.py:76
  94.4 3.8 %collective-permute-start.5 = (f32[4,2,512]{2,0,1:T(4,128)S(1)}, f32[4,2,512]{2,0,1:T(4,128)S(1)}, u32[]{:S(2)}, u32[]{:S(2)}) collective-permute-start(f32[4,2,512]{2,0,1:T(4,128)S(1)} %pad_maximum_fusion.5), channel_id=1, source_target_pairs={{0,2},{1,3},{2,0},{3,1},{4,6},{5,7},{6,4},{7,5},{8,10},{9,11},{10,... | collective-permute-start | bytes 49160 | tf_op jit(solution)/shard_map/ppermute | solution.py:76
  98.9 15.0 %collective-permute-start.26 = (f32[4,2,512]{2,0,1:T(4,128)S(1)}, f32[4,2,512]{2,0,1:T(4,128)S(1)}, u32[]{:S(2)}, u32[]{:S(2)}) collective-permute-start(f32[4,2,512]{2,0,1:T(4,128)S(1)} %pad_maximum_fusion.6), channel_id=1, source_target_pairs={{0,8},{4,12},{8,0},{12,4},{16,24},{20,28},{24,16},{28,20},{1,9},{5... | collective-permute-start | bytes 49160 | tf_op jit(solution)/shard_map/ppermute | solution.py:76
  113.8 4.6 %collective-permute-start.20 = (f32[4,2,512]{2,0,1:T(4,128)S(1)}, f32[4,2,512]{2,0,1:T(4,128)S(1)}, u32[]{:S(2)}, u32[]{:S(2)}) collective-permute-start(f32[4,2,512]{2,0,1:T(4,128)S(1)} %pad_maximum_fusion.6), channel_id=1, source_target_pairs={{0,16},{4,20},{8,24},{12,28},{16,0},{20,4},{24,8},{28,12},{1,17},{... | collective-permute-start | bytes 49160 | tf_op jit(solution)/shard_map/ppermute | solution.py:76
  118.5 5.5 %collective-permute-start.14 = (f32[4,2,512]{2,0,1:T(4,128)S(1)}, f32[4,2,512]{2,0,1:T(4,128)S(1)}, u32[]{:S(2)}, u32[]{:S(2)}) collective-permute-start(f32[4,2,512]{2,0,1:T(4,128)S(1)} %pad_maximum_fusion.6), channel_id=1, source_target_pairs={{0,24},{4,28},{8,16},{12,20},{16,8},{20,12},{24,0},{28,4},{1,25},{... | collective-permute-start | bytes 49160 | tf_op jit(solution)/shard_map/ppermute | solution.py:76
  124.0 9.5 %collective-permute-start.12 = (f32[520,256]{1,0:T(8,128)}, f32[520,256]{1,0:T(8,128)S(1)}, u32[]{:S(2)}, u32[]{:S(2)}) collective-permute-start(f32[520,256]{1,0:T(8,128)} %collective-permute-done.10.refs_0_), channel_id=1, source_target_pairs={{0,2},{1,3},{2,0},{3,1},{4,6},{5,7},{6,4},{7,5},{8,10},{9,11},{10,... | collective-permute-start | bytes 1597448 | tf_op jit(solution)/shard_map/ppermute | solution.py:76
  124.0 11.8 %collective-permute-start.11 = (f32[520,256]{1,0:T(8,128)}, f32[520,256]{1,0:T(8,128)S(1)}, u32[]{:S(2)}, u32[]{:S(2)}) collective-permute-start(f32[520,256]{1,0:T(8,128)} %collective-permute-done.10.refs_0_), channel_id=1, source_target_pairs={{0,1},{1,0},{2,3},{3,2},{4,5},{5,4},{6,7},{7,6},{8,9},{9,8},{10,11... | collective-permute-start | bytes 1597448 | tf_op jit(solution)/shard_map/ppermute | solution.py:76
  128.4 10.3 %collective-permute-start.25 = (f32[264,256]{1,0:T(8,128)S(1)}, f32[264,256]{1,0:T(8,128)S(1)}, u32[]{:S(2)}, u32[]{:S(2)}) collective-permute-start(f32[264,256]{1,0:T(8,128)S(1)} %slice.339), channel_id=1, source_target_pairs={{0,1},{1,0},{2,3},{3,2},{4,5},{5,4},{6,7},{7,6},{8,9},{9,8},{10,11... | collective-permute-start | bytes 811016 | tf_op jit(solution)/shard_map/ppermute | solution.py:76
  130.2 41.0 %collective-permute-start.27 = (f32[256,256]{1,0:T(8,128)S(1)}, f32[256,256]{1,0:T(8,128)}, u32[]{:S(2)}, u32[]{:S(2)}) collective-permute-start(f32[256,256]{1,0:T(8,128)S(1)} %slice.344), channel_id=1, source_target_pairs={{0,2},{1,3},{2,0},{3,1},{4,6},{5,7},{6,4},{7,5},{8,10},{9,11},{10,... | collective-permute-start | bytes 786440 | tf_op jit(solution)/shard_map/ppermute | solution.py:76
  130.4 11.3 %collective-permute-start.19 = (f32[264,256]{1,0:T(8,128)S(1)}, f32[264,256]{1,0:T(8,128)S(1)}, u32[]{:S(2)}, u32[]{:S(2)}) collective-permute-start(f32[264,256]{1,0:T(8,128)S(1)} %slice.329), channel_id=1, source_target_pairs={{0,1},{1,0},{2,3},{3,2},{4,5},{5,4},{6,7},{7,6},{8,9},{9,8},{10,11... | collective-permute-start | bytes 811016 | tf_op jit(solution)/shard_map/ppermute | solution.py:76
  133.5 38.6 %collective-permute-start.21 = (f32[256,256]{1,0:T(8,128)}, f32[256,256]{1,0:T(8,128)}, u32[]{:S(2)}, u32[]{:S(2)}) collective-permute-start(f32[256,256]{1,0:T(8,128)} %slice.334), channel_id=1, source_target_pairs={{0,2},{1,3},{2,0},{3,1},{4,6},{5,7},{6,4},{7,5},{8,10},{9,11},{10,... | collective-permute-start | bytes 786440 | tf_op jit(solution)/shard_map/ppermute | solution.py:76
  135.9 8.7 %collective-permute-start.13 = (f32[264,256]{1,0:T(8,128)S(1)}, f32[264,256]{1,0:T(8,128)S(1)}, u32[]{:S(2)}, u32[]{:S(2)}) collective-permute-start(f32[264,256]{1,0:T(8,128)S(1)} %slice.319), channel_id=1, source_target_pairs={{0,1},{1,0},{2,3},{3,2},{4,5},{5,4},{6,7},{7,6},{8,9},{9,8},{10,11... | collective-permute-start | bytes 811016 | tf_op jit(solution)/shard_map/ppermute | solution.py:76
  138.8 34.4 %collective-permute-start.15 = (f32[256,256]{1,0:T(8,128)}, f32[256,256]{1,0:T(8,128)}, u32[]{:S(2)}, u32[]{:S(2)}) collective-permute-start(f32[256,256]{1,0:T(8,128)} %slice.324), channel_id=1, source_target_pairs={{0,2},{1,3},{2,0},{3,1},{4,6},{5,7},{6,4},{7,5},{8,10},{9,11},{10,... | collective-permute-start | bytes 786440 | tf_op jit(solution)/shard_map/ppermute | solution.py:76
  206.0 30.7 %collective-permute-start.28 = (f32[2560,256]{1,0:T(8,128)}, f32[2560,256]{1,0:T(8,128)}, u32[]{:S(2)}, u32[]{:S(2)}) collective-permute-start(f32[2560,256]{1,0:T(8,128)} %constant_dynamic-slice_fusion.6), channel_id=1, source_target_pairs={{0,4},{4,0},{8,12},{12,8},{16,20},{20,16},{24,28},{28,24},{1,5},{5... | collective-permute-start | bytes 7864328 | tf_op jit(solution)/shard_map/ppermute | solution.py:76
  208.9 17.2 %collective-permute-start.6 = (f32[2,256,256]{2,1,0:T(8,128)}, f32[2,256,256]{2,1,0:T(8,128)S(1)}, u32[]{:S(2)}, u32[]{:S(2)}) collective-permute-start(f32[2,256,256]{2,1,0:T(8,128)} %pad_maximum_fusion.3), channel_id=1, source_target_pairs={{0,1},{1,0},{2,3},{3,2},{4,5},{5,4},{6,7},{7,6},{8,9},{9,8},{10,11... | collective-permute-start | bytes 1572872 | tf_op jit(solution)/shard_map/ppermute | solution.py:76
  215.1 14.2 %collective-permute-start.8 = (f32[2,256,256]{2,1,0:T(8,128)}, f32[2,256,256]{2,1,0:T(8,128)S(1)}, u32[]{:S(2)}, u32[]{:S(2)}) collective-permute-start(f32[2,256,256]{2,1,0:T(8,128)} %stack.142), channel_id=1, source_target_pairs={{0,2},{1,3},{2,0},{3,1},{4,6},{5,7},{6,4},{7,5},{8,10},{9,11},{10,... | collective-permute-start | bytes 1572872 | tf_op jit(solution)/shard_map/ppermute | solution.py:76
  226.0 8.2 %collective-permute-start.7 = (f32[1,256,256]{2,1,0:T(8,128)S(1)}, f32[1,256,256]{2,1,0:T(8,128)S(1)}, u32[]{:S(2)}, u32[]{:S(2)}) collective-permute-start(f32[1,256,256]{2,1,0:T(8,128)S(1)} %slice_add_fusion.2), channel_id=1, source_target_pairs={{0,2},{1,3},{2,0},{3,1},{4,6},{5,7},{6,4},{7,5},{8,10},{9,11},{10,... | collective-permute-start | bytes 786440 | tf_op jit(solution)/shard_map/ppermute | solution.py:76
  229.4 6.4 %collective-permute-start.9 = (f32[1,256,256]{2,1,0:T(8,128)S(1)}, f32[1,256,256]{2,1,0:T(8,128)S(1)}, u32[]{:S(2)}, u32[]{:S(2)}) collective-permute-start(f32[1,256,256]{2,1,0:T(8,128)S(1)} %slice_add_fusion), channel_id=1, source_target_pairs={{0,1},{1,0},{2,3},{3,2},{4,5},{5,4},{6,7},{7,6},{8,9},{9,8},{10,11... | collective-permute-start | bytes 786440 | tf_op jit(solution)/shard_map/ppermute | solution.py:76
  (22 other events, 94.5 us)

commit v2 on v1

v2 whole, which is shorter than its diff:
```python
import functools

import jax
import jax.numpy as jnp
from jax import lax
from jax.experimental import pallas as pl
from jax.experimental.pallas import tpu as pltpu
from jax.sharding import PartitionSpec as P

TILE = 512
KMAX = 3
EXTRA = 8
STAT = 4
MIB = 1024 * 1024

very_low = -1e30
high, highest = lax.Precision.HIGH, lax.Precision.HIGHEST

smem = pl.BlockSpec(memory_space=pltpu.SMEM)
vmem = pl.BlockSpec(memory_space=pltpu.VMEM)
anywhere = pl.BlockSpec(memory_space=pl.ANY)


def dot(a, b, dims=((1,), (0,)), precision=high):
    return lax.dot_general(a, b, (dims, ((), ())), precision=precision, preferred_element_type=jnp.float32)


def cost(us):
    return pl.CostEstimate(flops=0, bytes_accessed=int(us * 3.0e6), transcendentals=0)


def pack_kernel(q_ref, pos_ref, lists_ref, out_ref):
    rows, width = q_ref.shape
    out_ref[:rows, :] = q_ref[...]
    out_ref[rows : rows + EXTRA, :] = jnp.zeros((EXTRA, width), jnp.float32)
    row = pos_ref[...].astype(jnp.float32)
    col = jnp.broadcast_to(row, (8, rows)).T[:, 0:1]
    at_row = lax.broadcasted_iota(jnp.int32, (rows, rows), 1)
    at_col = lax.broadcasted_iota(jnp.int32, (rows, rows), 0)
    before = (row < col) | ((row == col) & (at_row < at_col))
    rank = jnp.sum(before.astype(jnp.float32), axis=1, keepdims=True)
    placed = rank == at_row.astype(jnp.float32)
    sorted_pos = jnp.sum(jnp.where(placed, col, 0.0), axis=0, keepdims=True)
    sorted_at = jnp.sum(jnp.where(placed, at_col.astype(jnp.float32), 0.0), axis=0, keepdims=True)
    per = rows // width
    for first, values in ((0, row), (per, sorted_pos), (2 * per, sorted_at)):
        for i in range(per):
            out_ref[rows + first + i : rows + first + i + 1, :] = values[:, i * width : (i + 1) * width]
    out_ref[rows + 3 * per : rows + 3 * per + 1, :] = lists_ref[...].astype(jnp.float32)


def pack(queries, positive, tile_ids, counts):
    rows, width = queries.shape
    lists = jnp.concatenate([tile_ids.reshape(-1), counts.reshape(-1)])
    lists = jnp.pad(lists, (0, width - lists.shape[0])).reshape(1, width)
    return pl.pallas_call(
        pack_kernel,
        out_shape=jax.ShapeDtypeStruct((rows + EXTRA, width), jnp.float32),
        compiler_params=pltpu.CompilerParams(vmem_limit_bytes=24 * MIB),
        cost_estimate=cost(2),
        name="pack",
    )(queries, positive.reshape(1, rows), lists)


class Lists:
    def __init__(self, ref, rows, shard_at, n_shard):
        self.ref, self.rows, self.shard_at, self.n_shard = ref, rows, shard_at, n_shard
        self.width = ref.shape[2]
        self.per = rows // self.width
        self.shift = self.width.bit_length() - 1

    def entry(self, b, first, i):
        return self.ref[b, first + (i >> self.shift), i & (self.width - 1)]

    def sorted_pos(self, b, i):
        return self.entry(b, self.per, i).astype(jnp.int32)

    def place(self, b, i):
        return self.entry(b, 2 * self.per, i).astype(jnp.int32)

    def tile(self, b, k):
        return self.ref[b, 3 * self.per, self.shard_at * KMAX + k].astype(jnp.int32)

    def count(self, b):
        return self.ref[b, 3 * self.per, self.n_shard * KMAX + self.shard_at].astype(jnp.int32)

    def first_from(self, b, start):
        def halve(_, ends):
            low, top = ends
            mid = (low + top) >> 1
            below = (low < top) & (self.sorted_pos(b, jnp.minimum(mid, self.rows - 1)) < start)
            return jnp.where(below, mid + 1, low), jnp.where(below | (low >= top), top, mid)

        return lax.fori_loop(0, self.rows.bit_length(), halve, (jnp.int32(0), jnp.int32(self.rows)))[0]


def swap(x, axis, bits):
    return lax.ppermute(x, axis, [(i, i ^ bits) for i in range(lax.axis_size(axis))])


def after(x, *others):
    return lax.optimization_barrier((x, *others))[0]


def plane(message, by_top):
    slots = [message]
    for j in range(1, lax.axis_size("shard")):
        bit = 1 << (j.bit_length() - 1) if by_top else j & -j
        slots.append(swap(slots[j ^ bit], "shard", bit))
    return slots


def stats_kernel(n, n_before, n_shard, at, *refs):
    msgs, refs = refs[:n], refs[n:]
    befores, refs = refs[:n_before], refs[n_before:]
    items_hbm, acc_ref, chosen_ref, stat_ref, q_ref, tiles, rowbuf, lists_ref, sems, row_sems = refs
    rows = q_ref.shape[1] - EXTRA
    width = q_ref.shape[2]
    per = rows // width
    lists = Lists(lists_ref, rows, at[0], n_shard)
    base, local_rows = at[1], items_hbm.shape[0]

    def get_lists(j):
        return pltpu.make_async_copy(msgs[j].at[rows : rows + EXTRA], lists_ref.at[j], sems.at[0, j])

    def get_q(j):
        return pltpu.make_async_copy(msgs[j], q_ref.at[j], sems.at[1, j])

    def get_tile(b, k):
        start = pl.multiple_of(lists.tile(b, k) * TILE, TILE)
        return pltpu.make_async_copy(items_hbm.at[pl.ds(start, TILE)], tiles.at[b * KMAX + k], sems.at[2 + k, b])

    def get_row(b, i):
        return pltpu.make_async_copy(
            items_hbm.at[pl.ds(lists.sorted_pos(b, i) - base, 1)], rowbuf.at[b, pl.ds(lists.place(b, i), 1)], row_sems.at[b]
        )

    for j in range(n):
        get_lists(j).start()
    for j in range(n):
        get_q(j).start()
    first = 0
    for before in befores:
        stat_ref[first : first + before.shape[0]] = before[...]
        first += before.shape[0]
    rowbuf[...] = jnp.zeros(rowbuf.shape, jnp.float32)
    for j in range(n):
        get_lists(j).wait()

    @pl.loop(0, n)
    def _(b):
        @pl.loop(0, lists.count(b))
        def _(k):
            get_tile(b, k).start()

    spans = []
    for b in range(n):
        spans.append((lists.first_from(b, base), lists.first_from(b, base + local_rows)))

        @pl.loop(*spans[b])
        def _(i):
            get_row(b, i).start()

    for j in range(n):
        get_q(j).wait()

    @pl.loop(0, n)
    def _(b):
        q_t = q_ref[b, :rows, :].T
        acc_ref[b] = jnp.zeros(acc_ref.shape[1:], jnp.float32)

        def visit(k, carry):
            top, total = carry
            get_tile(b, k).wait()
            tile = tiles[b * KMAX + k]
            logits = dot(tile, q_t, precision=highest)
            new_top = jnp.maximum(top, jnp.max(logits, axis=0, keepdims=True))
            prob = jnp.exp(logits - new_top)
            scale = jnp.exp(top - new_top)
            total = total * scale + jnp.sum(prob, axis=0, keepdims=True)
            acc_ref[b] = acc_ref[b] * scale + dot(tile.T, prob)
            return new_top, total

        start = (jnp.full((1, rows), very_low, jnp.float32), jnp.zeros((1, rows), jnp.float32))
        top, total = lax.fori_loop(0, lists.count(b), visit, start)
        stat_ref[first + b, 0:1, :] = top
        stat_ref[first + b, 1:2, :] = total

    for b in range(n):

        @pl.loop(*spans[b])
        def _(i):
            get_row(b, i).wait()

    @pl.loop(0, n)
    def _(b):
        chosen = rowbuf[b].T
        chosen_ref[b] = chosen
        pos = jnp.concatenate([q_ref[b, rows + i : rows + i + 1, :] for i in range(per)], axis=1).astype(jnp.int32)
        offset = pos - base
        inside = (offset >= 0) & (offset < local_rows)
        plogit = jnp.sum(q_ref[b, :rows, :].T * chosen, axis=0, keepdims=True)
        top, total = stat_ref[first + b, 0:1, :], stat_ref[first + b, 1:2, :]
        new_top = jnp.maximum(top, jnp.where(inside, plogit, very_low))
        total = total * jnp.exp(top - new_top) + jnp.where(inside, jnp.exp(plogit - new_top), 0.0)
        stat_ref[first + b, 1:2, :] = new_top + jnp.log(total)
        stat_ref[first + b, 2:3, :] = jnp.where(inside, plogit, 0.0)
        stat_ref[first + b, 3:4, :] = jnp.where(inside, 1.0, 0.0)


def stats(messages, befores, items, at):
    n = len(messages)
    rows, width = messages[0].shape[0] - EXTRA, messages[0].shape[1]
    total = n + sum(b.shape[0] for b in befores)
    sums = jax.ShapeDtypeStruct((n, width, rows), jnp.float32)
    return pl.pallas_call(
        functools.partial(stats_kernel, n, len(befores), lax.axis_size("shard")),
        out_shape=(sums, sums, jax.ShapeDtypeStruct((total, STAT, rows), jnp.float32)),
        in_specs=[smem] + [anywhere] * n + [vmem] * len(befores) + [anywhere],
        out_specs=(vmem, vmem, vmem),
        scratch_shapes=[
            pltpu.VMEM((n, rows + EXTRA, width), jnp.float32),
            pltpu.VMEM((n * KMAX, TILE, width), jnp.float32),
            pltpu.VMEM((n, rows, width), jnp.float32),
            pltpu.SMEM((n, EXTRA, width), jnp.float32),
            pltpu.SemaphoreType.DMA((2 + KMAX, n)),
            pltpu.SemaphoreType.DMA((n,)),
        ],
        compiler_params=pltpu.CompilerParams(vmem_limit_bytes=40 * MIB),
        cost_estimate=cost(5 * n),
        name="stats",
    )(at, *messages, *befores, items)


def dq_kernel(n, counts, *refs):
    stat_refs, refs = refs[:n], refs[n:]
    acc_refs, refs = refs[: len(counts)], refs[len(counts) :]
    chosen_refs, refs = refs[: len(counts)], refs[len(counts) :]
    loss_ref, term_ref, share_refs = refs[0], refs[1], refs[2:]
    b = 0
    for acc_ref, chosen_ref, count in zip(acc_refs, chosen_refs, counts):
        for i in range(count):
            parts = [stat_refs[j][b ^ j, 1:2, :] for j in range(n)]
            top = functools.reduce(jnp.maximum, parts)
            lse = top + jnp.log(sum(jnp.exp(p - top) for p in parts))
            plogit = sum(stat_refs[j][b ^ j, 2:3, :] for j in range(n))
            weight = jnp.exp(plogit - lse) - 1.0
            term_ref[0, b : b + 1, :] = lse
            term_ref[1, b : b + 1, :] = weight
            if b == 0:
                loss_ref[...] = lse - plogit
            own = stat_refs[0]
            share = acc_ref[i] * jnp.exp(own[b, 0:1, :] - lse) + chosen_ref[i] * (weight * own[b, 3:4, :])
            share_refs[b][...] = share.T
            b += 1


def dq_shares(all_stats, accs, chosens):
    n, _, rows = all_stats[0].shape
    width = accs[0].shape[1]
    share = jax.ShapeDtypeStruct((rows, width), jnp.float32)
    out = pl.pallas_call(
        functools.partial(dq_kernel, n, [a.shape[0] for a in accs]),
        out_shape=(
            jax.ShapeDtypeStruct((1, rows), jnp.float32),
            jax.ShapeDtypeStruct((2, n, rows), jnp.float32),
            *[share] * n,
        ),
        compiler_params=pltpu.CompilerParams(vmem_limit_bytes=40 * MIB),
        cost_estimate=cost(3),
        name="dq",
    )(*all_stats, *accs, *chosens)
    return out[0], out[1], out[2:]


def item_kernel(n, n_shard, is_first, is_last, at, weight, *refs):
    msgs, refs = refs[:n], refs[n:]
    lse_ref, items_hbm, refs = refs[0], refs[1], refs[2:]
    if not is_first:
        acc_hbm, refs = refs[0], refs[1:]
    outs, refs = refs[: 1 + is_last], refs[1 + is_last :]
    q_ref, items, acc, lists_ref, sems = refs
    rows, width = q_ref.shape[1], q_ref.shape[2]
    span_rows = acc.shape[0]
    tiles = span_rows // TILE
    base, first_tile, core = at[1] + at[2] * TILE, at[2], at[3]
    lists = Lists(lists_ref, rows, at[0], n_shard)
    start = pl.multiple_of(first_tile * TILE, TILE)
    get_items = pltpu.make_async_copy(items_hbm.at[pl.ds(start, span_rows)], items, sems.at[2, 0])

    def get_lists(j):
        return pltpu.make_async_copy(msgs[j].at[rows : rows + EXTRA], lists_ref.at[j], sems.at[0, j])

    def get_q(j):
        return pltpu.make_async_copy(msgs[j].at[:rows], q_ref.at[j], sems.at[1, j])

    for j in range(n):
        get_lists(j).start()
    if is_first:
        get_items.start()
        acc[...] = jnp.zeros(acc.shape, jnp.float32)
    else:
        get_acc = pltpu.make_async_copy(acc_hbm, acc, sems.at[2, 1])
        get_acc.start()
        get_items.start()
    for j in range(n):
        get_q(j).start()
    for j in range(n):
        get_lists(j).wait()
    if not is_first:
        get_acc.wait()
    for j in range(n):
        get_q(j).wait()

    @pl.loop(0, n)
    def _(b):
        @pl.loop(lists.first_from(b, base), lists.first_from(b, base + span_rows))
        def _(i):
            place = lists.place(b, i)
            here = pl.ds(lists.sorted_pos(b, i) - base, 1)
            acc[here, :] += q_ref[b, pl.ds(place, 1), :] * weight[1, b, place]

    get_items.wait()

    @pl.loop(0, n)
    def _(b):
        @pl.loop(0, lists.count(b))
        def _(k):
            tile = lists.tile(b, k) - first_tile

            @pl.when((tile >= 0) & (tile < tiles))
            def _():
                here = pl.ds(pl.multiple_of(tile * TILE, TILE), TILE)
                q = q_ref[b]
                logits = dot(items[here, :], q, ((1,), (1,)), highest)
                prob = jnp.exp(logits - lse_ref[0, pl.ds(b, 1), :])
                acc[here, :] += dot(prob, q)

    if is_last:
        own = span_rows // 2
        mine, other = outs
        put = [
            pltpu.make_async_copy(acc.at[pl.ds(pl.multiple_of((1 - core) * own, 8), own)], other, sems.at[2, 0]),
            pltpu.make_async_copy(acc.at[pl.ds(pl.multiple_of(core * own, 8), own)], mine, sems.at[2, 1]),
        ]
    else:
        put = [pltpu.make_async_copy(acc, outs[0], sems.at[2, 0])]
    for p in put:
        p.start()
    for p in put:
        p.wait()


def item_grads(messages, terms, items, acc, span_rows, at, is_last):
    n = len(messages)
    rows, width = messages[0].shape[0] - EXTRA, messages[0].shape[1]
    is_first = acc is None
    half = jax.ShapeDtypeStruct((span_rows // 2, width), jnp.float32)
    whole = jax.ShapeDtypeStruct((span_rows, width), jnp.float32)
    carried = [] if is_first else [acc]
    return pl.pallas_call(
        functools.partial(item_kernel, n, lax.axis_size("shard"), is_first, is_last),
        out_shape=(half, half) if is_last else whole,
        in_specs=[smem] * 2 + [anywhere] * n + [vmem, anywhere] + [anywhere] * len(carried),
        out_specs=(anywhere, anywhere) if is_last else anywhere,
        scratch_shapes=[
            pltpu.VMEM((n, rows, width), jnp.float32),
            pltpu.VMEM((span_rows, width), jnp.float32),
            pltpu.VMEM((span_rows, width), jnp.float32),
            pltpu.SMEM((n, EXTRA, width), jnp.float32),
            pltpu.SemaphoreType.DMA((3, max(n, 2))),
        ],
        compiler_params=pltpu.CompilerParams(vmem_limit_bytes=32 * MIB),
        cost_estimate=cost(2 * n),
        name="item_grads",
    )(at, terms, *messages, terms, items, *carried)


def local(queries, items, positive, tile_ids, counts):
    dp_at, shard_at = lax.axis_index("dp"), lax.axis_index("shard")
    n_dp, n_shard = lax.axis_size("dp"), lax.axis_size("shard")
    rows, width = queries.shape
    local_rows = items.shape[0]
    span_rows = 2 * (local_rows // n_dp)
    n_chips = n_dp // 2
    at = jnp.stack([shard_at, shard_at * local_rows, (dp_at // 2) * (span_rows // TILE), dp_at % 2]).astype(jnp.int32)

    message = pack(queries, positive, tile_ids, counts)
    group = plane(message, True)
    near = [swap(m, "dp", 2) for m in group]
    far, last = [], near[0]
    for k in range(2, n_chips):
        last = swap(after(message, last), "dp", 2 * k)
        far.append(last)
    groups = [group, near] + [plane(m, i % 2 == 0) for i, m in enumerate(far)]

    acc0, chosen0, stat0 = stats(group[:1], [], items, at)
    acc1, chosen1, stat1 = stats(group[1:3], [stat0], items, at)
    acc2, chosen2, stat = stats(group[3:], [stat1], items, at)
    all_stats = [stat] + [swap(stat, "shard", j) for j in range(1, n_shard)]
    loss, sent, shares = dq_shares(all_stats, [acc0, acc1, acc2], [chosen0, chosen1, chosen2])

    terms = [sent] + [swap(sent, "dp", 2 * k) for k in range(1, n_chips)]
    query_grad = shares[0] + sum(swap(shares[j], "shard", j) for j in range(1, n_shard))

    grads = None
    for k in range(n_chips):
        grads = item_grads(groups[k], terms[k], items, grads, span_rows, at, k == n_chips - 1)
    mine, other = grads
    item_grad = mine + swap(other, "dp", 1)
    return loss.reshape(rows), query_grad, item_grad


def solution(mesh):
    placed = (
        P(("dp", "shard"), None),
        P("shard", None),
        P(("dp", "shard")),
        P(("dp", "shard"), None, None),
        P(("dp", "shard"), None),
    )
    return jax.shard_map(
        local,
        mesh=mesh,
        in_specs=placed,
        out_specs=(P(("dp", "shard")), P(("dp", "shard"), None), P(("shard", "dp"), None)),
        check_vma=False,
    )
```

time: 245 us -> 221 us (0.902); the launches traced: 241 us -> 222 us
  local copies, waits for them, and re-layouts: 46.8 us -> 2.58 us
  waiting for transfers between devices: 56.5 us -> 81.9 us
  other arithmetic: 25.5 us -> 3.56 us
  Pallas kernels: 64.2 us -> 78.3 us
  starting transfers between devices: 46.9 us -> 54.5 us
    ppermute x29 -> x25, waiting for transfers between devices: 56.5 us -> 81.9 us  [swap(): lax.ppermute(x, axis, [(i, i ^ bits) for i in range(lax.axis_size(axis))])]
    unnamed x65 -> x5, local copies, waits for them, and re-layouts: 21.7 us -> 2.49 us
    pallas_call x6 -> x8, Pallas kernels: 63.7 us -> 77.8 us  [the longest x3 38.4 us: stats(): pl.pallas_call(functools.partial(stats_kernel, n, len(befores), lax.axis_...]
    another operation x27 -> x0, local copies, waits for them, and re-layouts: 12.9 us -> none  [the longest x10 8.03 us: span(): jnp.stack([jnp.sum(sorted_pos < start, axis=1), jnp.sum(sorted_pos < star...]
    ppermute x29 -> x25, starting transfers between devices: 46.9 us -> 54.5 us  [swap(): lax.ppermute(x, axis, [(i, i ^ bits) for i in range(lax.axis_size(axis))])]
    slice x20 -> x0, local copies, waits for them, and re-layouts: 5.73 us -> none  [the longest x4 2.43 us: plane(): first = swap(slots[j ^ top_bit][:half], 'shard', top_bit)]
    unnamed x8 -> x0, other arithmetic: 5.02 us -> none
    another operation x9 -> x1, other arithmetic: 3.98 us -> 0.08 us  [local(): jnp.stack([shard_at, shard_at * local_rows, dp_at // 2 * (span_rows // TI...]
  transfers between devices with their start and end apart: 29 -> 25, of which waited for: 16 -> 12; matrix products, arithmetic and copies ran while one was open for 20% -> 0% of each run, Pallas kernels for 16% -> 30%
where the time goes in v2:
time: 221 us; the launch traced here: 222 us
  waiting for transfers between devices  81.9 us (37%)
  Pallas kernels  78.3 us (35%)
  starting transfers between devices  54.5 us (25%)
  other arithmetic  3.56 us (2%)
  local copies, waits for them, and re-layouts  2.58 us (1%)
    ppermute x25, waiting for transfers between devices, swap(): lax.ppermute(x, axis, [(i, i ^ bits) for i in range(lax.axis_size(axis))])  81.9 us
    ppermute x25, starting transfers between devices, swap(): lax.ppermute(x, axis, [(i, i ^ bits) for i in range(lax.axis_size(axis))])  54.5 us
    pallas_call x3, Pallas kernels, stats(): pl.pallas_call(functools.partial(stats_kernel, n, len(befores), lax.axis_...  38.4 us
    pallas_call x4, Pallas kernels, item_grads(): pl.pallas_call(functools.partial(item_kernel, n, lax.axis_size('shard'),...  38.2 us
  transfers between devices with their start and end apart: 25, of which 12 were waited for; matrix products, arithmetic and copies ran while one was open for 0% of the time, Pallas kernels for 30%

profile of v2, /device:TPU:0, one launch (start us, length us, event | category | flops | bytes accessed | tf_op | source)
XLA Modules:
  0.0 221.7 jit_solution(8198245223400976635)
XLA Ops:
  4.5 3.1 %collective-permute-start.10 = (f32[520,256]{1,0:T(8,128)S(1)}, f32[520,256]{1,0:T(8,128)S(1)}, u32[]{:S(2)}, u32[]{:S(2)}) collective-permute-start(f32[520,256]{1,0:T(8,128)S(1)} %pack.1.refs_0_), channel_id=1, source_target_pairs={{0,8},{4,12},{8,0},{12,4},{16,24},{20,28},{24,16},{28,20},{1,9},{5... | collective-permute-start | bytes 1597448 | tf_op jit(solution)/shard_map/ppermute | solution.py:98
  7.6 12.1 %collective-permute-done.10.refs_0_ = f32[520,256]{1,0:T(8,128)S(1)} collective-permute-done((f32[520,256]{1,0:T(8,128)S(1)}, f32[520,256]{1,0:T(8,128)S(1)}, u32[]{:S(2)}, u32[]{:S(2)}) %collective-permute-start.10) | collective-permute-done | bytes 532512 | tf_op jit(solution)/shard_map/ppermute | solution.py:98
  19.7 2.8 %collective-permute-start.11 = (f32[520,256]{1,0:T(8,128)S(1)}, f32[520,256]{1,0:T(8,128)S(1)}, u32[]{:S(2)}, u32[]{:S(2)}) collective-permute-start(f32[520,256]{1,0:T(8,128)S(1)} %pack.1.refs_0_), channel_id=1, source_target_pairs={{0,16},{4,20},{8,24},{12,28},{16,0},{20,4},{24,8},{28,12},{1,17},{... | collective-permute-start | bytes 1597448 | tf_op jit(solution)/shard_map/ppermute | solution.py:98
  23.9 1.5 collective-permute-start.2
  25.4 19.8 %collective-permute-done.11.refs_0_ = f32[520,256]{1,0:T(8,128)S(1)} collective-permute-done((f32[520,256]{1,0:T(8,128)S(1)}, f32[520,256]{1,0:T(8,128)S(1)}, u32[]{:S(2)}, u32[]{:S(2)}) %collective-permute-start.11) | collective-permute-done | bytes 532512 | tf_op jit(solution)/shard_map/ppermute | solution.py:98
  45.3 3.3 %collective-permute-start.12 = (f32[520,256]{1,0:T(8,128)S(1)}, f32[520,256]{1,0:T(8,128)}, u32[]{:S(2)}, u32[]{:S(2)}) collective-permute-start(f32[520,256]{1,0:T(8,128)S(1)} %pack.1.refs_0_), channel_id=1, source_target_pairs={{0,24},{4,28},{8,16},{12,20},{16,8},{20,12},{24,0},{28,4},{1,25},{... | collective-permute-start | bytes 1597448 | tf_op jit(solution)/shard_map/ppermute | solution.py:98
  48.6 1.5 collective-permute-start.1
  50.1 2.0 collective-permute-start.22
  52.2 1.5 collective-permute-start.17
  53.7 8.6 %collective-permute-done.12.refs_0_ = f32[520,256]{1,0:T(8,128)} collective-permute-done((f32[520,256]{1,0:T(8,128)S(1)}, f32[520,256]{1,0:T(8,128)}, u32[]{:S(2)}, u32[]{:S(2)}) %collective-permute-start.12) | collective-permute-done | bytes 532512 | tf_op jit(solution)/shard_map/ppermute | solution.py:98
  63.6 9.6 %stats.3 = (f32[1,256,512]{2,1,0:T(8,128)S(1)}, f32[1,256,512]{2,1,0:T(8,128)S(1)}, f32[1,4,512]{2,1,0:T(4,128)S(1)}) custom-call(s32[4]{0:T(128)S(1)} %pad_add_fusion.at, f32[520,256]{1,0:T(8,128)S(1)} %pack.1.refs_0_, f32[20480,256]{1,0:T(8,128)} %refs_5_.7), custom_call_target="tpu_custom_call" | custom-call | bytes 15000000 | tf_op jit(solution)/shard_map/stats/pallas_call | solution.py:216
  73.2 18.1 %stats.4 = (f32[2,256,512]{2,1,0:T(8,128)S(1)}, f32[2,256,512]{2,1,0:T(8,128)S(1)}, f32[3,4,512]{2,1,0:T(4,128)S(1)}) custom-call(s32[4]{0:T(128)S(1)} %pad_add_fusion.at, f32[520,256]{1,0:T(8,128)S(1)} %collective-permute-done.refs_0_.refs_1_, f32[520,256]{1,0:T(8,128)S(1)} %collective-permute-done.2.refs_1_.refs_2_, ...), custom_call_target="tpu_custom_call" | custom-call | bytes 30000000 | tf_op jit(solution)/shard_map/stats/pallas_call | solution.py:216
  91.3 10.7 %stats.5 = (f32[1,256,512]{2,1,0:T(8,128)S(1)}, f32[1,256,512]{2,1,0:T(8,128)S(1)}, f32[4,4,512]{2,1,0:T(4,128)S(1)}) custom-call(s32[4]{0:T(128)S(1)} %pad_add_fusion.at, f32[520,256]{1,0:T(8,128)S(1)} %collective-permute-done.1.refs_0_.refs_3_, f32[3,4,512]{2,1,0:T(4,128)S(1)} %get-tuple-element.23.refs_1_, f32[20480,256]{1,0:T(8,128)} %refs_5_.7), custom_call_target="tpu_custom_call" | custom-call | bytes 15000000 | tf_op jit(solution)/shard_map/stats/pallas_call | solution.py:216
  102.1 3.9 %collective-permute-done.3.refs_1_ = f32[4,4,512]{2,1,0:T(4,128)S(1)} collective-permute-done((f32[4,4,512]{2,1,0:T(4,128)S(1)}, f32[4,4,512]{2,1,0:T(4,128)S(1)}, u32[]{:S(2)}, u32[]{:S(2)}) %collective-permute-start.3) | collective-permute-done | bytes 32800 | tf_op jit(solution)/shard_map/ppermute | solution.py:98
  106.1 3.9 %collective-permute-done.4.refs_2_ = f32[4,4,512]{2,1,0:T(4,128)S(1)} collective-permute-done((f32[4,4,512]{2,1,0:T(4,128)S(1)}, f32[4,4,512]{2,1,0:T(4,128)S(1)}, u32[]{:S(2)}, u32[]{:S(2)}) %collective-permute-start.4) | collective-permute-done | bytes 32800 | tf_op jit(solution)/shard_map/ppermute | solution.py:98
  110.0 4.8 %collective-permute-done.5.refs_3_ = f32[4,4,512]{2,1,0:T(4,128)S(1)} collective-permute-done((f32[4,4,512]{2,1,0:T(4,128)S(1)}, f32[4,4,512]{2,1,0:T(4,128)S(1)}, u32[]{:S(2)}, u32[]{:S(2)}) %collective-permute-start.5) | collective-permute-done | bytes 32800 | tf_op jit(solution)/shard_map/ppermute | solution.py:98
  115.9 11.8 %collective-permute-start.20 = (f32[2,4,512]{2,1,0:T(4,128)S(1)}, f32[2,4,512]{2,1,0:T(4,128)S(1)}, u32[]{:S(2)}, u32[]{:S(2)}) collective-permute-start(f32[2,4,512]{2,1,0:T(4,128)S(1)} %get-tuple-element.36.weight.refs_4_), channel_id=1, source_target_pairs={{0,8},{4,12},{8,0},{12,4},{16,24},{20,28},{24,16},{28,20},{1,9},{5... | collective-permute-start | bytes 49160 | tf_op jit(solution)/shard_map/ppermute | solution.py:98
  127.8 1.6 collective-permute-done.20.weight.refs_4_
  129.9 1.6 collective-permute-start.19
  131.5 3.4 %collective-permute-done.16.weight.refs_4_ = f32[2,4,512]{2,1,0:T(4,128)S(1)} collective-permute-done((f32[2,4,512]{2,1,0:T(4,128)S(1)}, f32[2,4,512]{2,1,0:T(4,128)S(1)}, u32[]{:S(2)}, u32[]{:S(2)}) %collective-permute-start.16) | collective-permute-done | bytes 16416 | tf_op jit(solution)/shard_map/ppermute | solution.py:98
  134.8 1.9 collective-permute-start.13
  137.2 2.8 %collective-permute-start.9 = (f32[2,4,512]{2,1,0:T(4,128)S(1)}, f32[2,4,512]{2,1,0:T(4,128)S(1)}, u32[]{:S(2)}, u32[]{:S(2)}) collective-permute-start(f32[2,4,512]{2,1,0:T(4,128)S(1)} %get-tuple-element.36.weight.refs_4_), channel_id=1, source_target_pairs={{0,24},{4,28},{8,16},{12,20},{16,8},{20,12},{24,0},{28,4},{1,25},{... | collective-permute-start | bytes 49160 | tf_op jit(solution)/shard_map/ppermute | solution.py:98
  140.0 6.9 %item_grads.4.refs_6_ = f32[5120,256]{1,0:T(8,128)S(1)} custom-call(s32[4]{0:T(128)S(1)} %pad_add_fusion.at, f32[2,4,512]{2,1,0:T(4,128)S(1)} %get-tuple-element.36.weight.refs_4_, f32[520,256]{1,0:T(8,128)S(1)} %pack.1.refs_0_, f32[520,256]{1,0:T(8,128)S(1)} %collective-permute-done.refs_0_.refs_1_, f32[520,256]{1,0:T(8,128)S(1)} %collective-permute-done.2.refs_1_.refs_2_, ...), custom_call_target="tpu_custom_call" | custom-call | bytes 24000000 | tf_op jit(solution)/shard_map/item_grads/pallas_call | solution.py:361
  146.9 9.0 %item_grads.5.refs_6_ = f32[5120,256]{1,0:T(8,128)S(1)} custom-call(s32[4]{0:T(128)S(1)} %pad_add_fusion.at, f32[2,4,512]{2,1,0:T(4,128)S(1)} %collective-permute-done.20.weight.refs_4_, f32[520,256]{1,0:T(8,128)S(1)} %collective-permute-done.10.refs_0_, f32[520,256]{1,0:T(8,128)} %collective-permute-done.21.refs_1_, ...), custom_call_target="tpu_custom_call" | custom-call | bytes 24000000 | tf_op jit(solution)/shard_map/item_grads/pallas_call | solution.py:361
  155.8 10.1 %item_grads.6.refs_6_ = f32[5120,256]{1,0:T(8,128)S(1)} custom-call(s32[4]{0:T(128)S(1)} %pad_add_fusion.at, f32[2,4,512]{2,1,0:T(4,128)S(1)} %collective-permute-done.16.weight.refs_4_, f32[520,256]{1,0:T(8,128)S(1)} %collective-permute-done.11.refs_0_, f32[520,256]{1,0:T(8,128)} %collective-permute-done.17.refs_1_, ...), custom_call_target="tpu_custom_call" | custom-call | bytes 24000000 | tf_op jit(solution)/shard_map/item_grads/pallas_call | solution.py:361
  165.9 12.4 %item_grads.7 = (f32[2560,256]{1,0:T(8,128)S(1)}, f32[2560,256]{1,0:T(8,128)S(1)}) custom-call(s32[4]{0:T(128)S(1)} %pad_add_fusion.at, f32[2,4,512]{2,1,0:T(4,128)S(1)} %collective-permute-done.9.weight.refs_4_, f32[520,256]{1,0:T(8,128)} %collective-permute-done.12.refs_0_, f32[520,256]{1,0:T(8,128)S(1)} %collective-permute-done.13.refs_1_, ...), custom_call_target="tpu_custom_call" | custom-call | bytes 24000000 | tf_op jit(solution)/shard_map/item_grads/pallas_call | solution.py:361
  178.3 8.0 %collective-permute-start.24 = (f32[2560,256]{1,0:T(8,128)S(1)}, f32[2560,256]{1,0:T(8,128)S(1)}, u32[]{:S(2)}, u32[]{:S(2)}) collective-permute-start(f32[2560,256]{1,0:T(8,128)S(1)} %get-tuple-element.40), channel_id=1, source_target_pairs={{0,4},{4,0},{8,12},{12,8},{16,20},{20,16},{24,28},{28,24},{1,5},{5... | collective-permute-start | bytes 7864328 | tf_op jit(solution)/shard_map/ppermute | solution.py:98
  186.3 7.7 %collective-permute-start.7 = (f32[512,256]{1,0:T(8,128)S(1)}, f32[512,256]{1,0:T(8,128)S(1)}, u32[]{:S(2)}, u32[]{:S(2)}) collective-permute-start(f32[512,256]{1,0:T(8,128)S(1)} %get-tuple-element.34), channel_id=1, source_target_pairs={{0,2},{1,3},{2,0},{3,1},{4,6},{5,7},{6,4},{7,5},{8,10},{9,11},{10,... | collective-permute-start | bytes 1572872 | tf_op jit(solution)/shard_map/ppermute | solution.py:98
  195.5 5.6 %collective-permute-done.6 = f32[512,256]{1,0:T(8,128)S(1)} collective-permute-done((f32[512,256]{1,0:T(8,128)S(1)}, f32[512,256]{1,0:T(8,128)S(1)}, u32[]{:S(2)}, u32[]{:S(2)}) %collective-permute-start.6) | collective-permute-done | bytes 524320 | tf_op jit(solution)/shard_map/ppermute | solution.py:98
  201.1 15.9 %collective-permute-done.7 = f32[512,256]{1,0:T(8,128)S(1)} collective-permute-done((f32[512,256]{1,0:T(8,128)S(1)}, f32[512,256]{1,0:T(8,128)S(1)}, u32[]{:S(2)}, u32[]{:S(2)}) %collective-permute-start.7) | collective-permute-done | bytes 524320 | tf_op jit(solution)/shard_map/ppermute | solution.py:98
  217.0 1.9 collective-permute-done.8
  219.9 1.8 add.23
  (38 shorter events, 11.3 us)
Async XLA Ops:
  2.2 1.0 copy-start
  3.3 0.7 copy-start.1
  4.5 15.2 %collective-permute-start.10 = (f32[520,256]{1,0:T(8,128)S(1)}, f32[520,256]{1,0:T(8,128)S(1)}, u32[]{:S(2)}, u32[]{:S(2)}) collective-permute-start(f32[520,256]{1,0:T(8,128)S(1)} %pack.1.refs_0_), channel_id=1, source_target_pairs={{0,8},{4,12},{8,0},{12,4},{16,24},{20,28},{24,16},{28,20},{1,9},{5... | collective-permute-start | bytes 1597448 | tf_op jit(solution)/shard_map/ppermute | solution.py:98
  19.7 25.6 %collective-permute-start.11 = (f32[520,256]{1,0:T(8,128)S(1)}, f32[520,256]{1,0:T(8,128)S(1)}, u32[]{:S(2)}, u32[]{:S(2)}) collective-permute-start(f32[520,256]{1,0:T(8,128)S(1)} %pack.1.refs_0_), channel_id=1, source_target_pairs={{0,16},{4,20},{8,24},{12,28},{16,0},{20,4},{24,8},{28,12},{1,17},{... | collective-permute-start | bytes 1597448 | tf_op jit(solution)/shard_map/ppermute | solution.py:98
  22.4 26.2 %collective-permute-start = (f32[520,256]{1,0:T(8,128)S(1)}, f32[520,256]{1,0:T(8,128)S(1)}, u32[]{:S(2)}, u32[]{:S(2)}) collective-permute-start(f32[520,256]{1,0:T(8,128)S(1)} %pack.1.refs_0_), channel_id=1, source_target_pairs={{0,1},{1,0},{2,3},{3,2},{4,5},{5,4},{6,7},{7,6},{8,9},{9,8},{10,11... | collective-permute-start | bytes 1597448 | tf_op jit(solution)/shard_map/ppermute | solution.py:98
  23.9 26.2 %collective-permute-start.2 = (f32[520,256]{1,0:T(8,128)S(1)}, f32[520,256]{1,0:T(8,128)S(1)}, u32[]{:S(2)}, u32[]{:S(2)}) collective-permute-start(f32[520,256]{1,0:T(8,128)S(1)} %pack.1.refs_0_), channel_id=1, source_target_pairs={{0,2},{1,3},{2,0},{3,1},{4,6},{5,7},{6,4},{7,5},{8,10},{9,11},{10,... | collective-permute-start | bytes 1597448 | tf_op jit(solution)/shard_map/ppermute | solution.py:98
  45.3 16.9 %collective-permute-start.12 = (f32[520,256]{1,0:T(8,128)S(1)}, f32[520,256]{1,0:T(8,128)}, u32[]{:S(2)}, u32[]{:S(2)}) collective-permute-start(f32[520,256]{1,0:T(8,128)S(1)} %pack.1.refs_0_), channel_id=1, source_target_pairs={{0,24},{4,28},{8,16},{12,20},{16,8},{20,12},{24,0},{28,4},{1,25},{... | collective-permute-start | bytes 1597448 | tf_op jit(solution)/shard_map/ppermute | solution.py:98
  48.6 42.7 %collective-permute-start.1 = (f32[520,256]{1,0:T(8,128)S(1)}, f32[520,256]{1,0:T(8,128)S(1)}, u32[]{:S(2)}, u32[]{:S(2)}) collective-permute-start(f32[520,256]{1,0:T(8,128)S(1)} %collective-permute-done.refs_0_.refs_1_), channel_id=1, source_target_pairs={{0,2},{1,3},{2,0},{3,1},{4,6},{5,7},{6,4},{7,5},{8,10},{9,11},{10,... | collective-permute-start | bytes 1597448 | tf_op jit(solution)/shard_map/ppermute | solution.py:98
  50.1 77.6 %collective-permute-start.21 = (f32[520,256]{1,0:T(8,128)S(1)}, f32[520,256]{1,0:T(8,128)}, u32[]{:S(2)}, u32[]{:S(2)}) collective-permute-start(f32[520,256]{1,0:T(8,128)S(1)} %collective-permute-done.refs_0_.refs_1_), channel_id=1, source_target_pairs={{0,8},{4,12},{8,0},{12,4},{16,24},{20,28},{24,16},{28,20},{1,9},{5... | collective-permute-start | bytes 1597448 | tf_op jit(solution)/shard_map/ppermute | solution.py:98
  50.1 77.6 %collective-permute-start.22 = (f32[520,256]{1,0:T(8,128)S(1)}, f32[520,256]{1,0:T(8,128)}, u32[]{:S(2)}, u32[]{:S(2)}) collective-permute-start(f32[520,256]{1,0:T(8,128)S(1)} %collective-permute-done.2.refs_1_.refs_2_), channel_id=1, source_target_pairs={{0,8},{4,12},{8,0},{12,4},{16,24},{20,28},{24,16},{28,20},{1,9},{5... | collective-permute-start | bytes 1597448 | tf_op jit(solution)/shard_map/ppermute | solution.py:98
  52.2 77.7 %collective-permute-start.17 = (f32[520,256]{1,0:T(8,128)S(1)}, f32[520,256]{1,0:T(8,128)}, u32[]{:S(2)}, u32[]{:S(2)}) collective-permute-start(f32[520,256]{1,0:T(8,128)S(1)} %collective-permute-done.11.refs_0_), channel_id=1, source_target_pairs={{0,1},{1,0},{2,3},{3,2},{4,5},{5,4},{6,7},{7,6},{8,9},{9,8},{10,11... | collective-permute-start | bytes 1597448 | tf_op jit(solution)/shard_map/ppermute | solution.py:98
  62.2 74.5 %collective-permute-start.14 = (f32[520,256]{1,0:T(8,128)}, f32[520,256]{1,0:T(8,128)}, u32[]{:S(2)}, u32[]{:S(2)}) collective-permute-start(f32[520,256]{1,0:T(8,128)} %collective-permute-done.12.refs_0_), channel_id=1, source_target_pairs={{0,2},{1,3},{2,0},{3,1},{4,6},{5,7},{6,4},{7,5},{8,10},{9,11},{10,... | collective-permute-start | bytes 1597448 | tf_op jit(solution)/shard_map/ppermute | solution.py:98
  102.1 4.0 %collective-permute-start.3 = (f32[4,4,512]{2,1,0:T(4,128)S(1)}, f32[4,4,512]{2,1,0:T(4,128)S(1)}, u32[]{:S(2)}, u32[]{:S(2)}) collective-permute-start(f32[4,4,512]{2,1,0:T(4,128)S(1)} %get-tuple-element.24.refs_0_), channel_id=1, source_target_pairs={{0,1},{1,0},{2,3},{3,2},{4,5},{5,4},{6,7},{7,6},{8,9},{9,8},{10,11... | collective-permute-start | bytes 98312 | tf_op jit(solution)/shard_map/ppermute | solution.py:98
  106.1 3.9 %collective-permute-start.4 = (f32[4,4,512]{2,1,0:T(4,128)S(1)}, f32[4,4,512]{2,1,0:T(4,128)S(1)}, u32[]{:S(2)}, u32[]{:S(2)}) collective-permute-start(f32[4,4,512]{2,1,0:T(4,128)S(1)} %get-tuple-element.24.refs_0_), channel_id=1, source_target_pairs={{0,2},{1,3},{2,0},{3,1},{4,6},{5,7},{6,4},{7,5},{8,10},{9,11},{10,... | collective-permute-start | bytes 98312 | tf_op jit(solution)/shard_map/ppermute | solution.py:98
  110.0 4.8 %collective-permute-start.5 = (f32[4,4,512]{2,1,0:T(4,128)S(1)}, f32[4,4,512]{2,1,0:T(4,128)S(1)}, u32[]{:S(2)}, u32[]{:S(2)}) collective-permute-start(f32[4,4,512]{2,1,0:T(4,128)S(1)} %get-tuple-element.24.refs_0_), channel_id=1, source_target_pairs={{0,3},{1,2},{2,1},{3,0},{4,7},{5,6},{6,5},{7,4},{8,11},{9,10},{10,... | collective-permute-start | bytes 98312 | tf_op jit(solution)/shard_map/ppermute | solution.py:98
  115.9 13.5 %collective-permute-start.20 = (f32[2,4,512]{2,1,0:T(4,128)S(1)}, f32[2,4,512]{2,1,0:T(4,128)S(1)}, u32[]{:S(2)}, u32[]{:S(2)}) collective-permute-start(f32[2,4,512]{2,1,0:T(4,128)S(1)} %get-tuple-element.36.weight.refs_4_), channel_id=1, source_target_pairs={{0,8},{4,12},{8,0},{12,4},{16,24},{20,28},{24,16},{28,20},{1,9},{5... | collective-permute-start | bytes 49160 | tf_op jit(solution)/shard_map/ppermute | solution.py:98
  127.7 9.4 %collective-permute-start.23 = (f32[520,256]{1,0:T(8,128)S(1)}, f32[520,256]{1,0:T(8,128)S(1)}, u32[]{:S(2)}, u32[]{:S(2)}) collective-permute-start(f32[520,256]{1,0:T(8,128)S(1)} %collective-permute-done.1.refs_0_.refs_3_), channel_id=1, source_target_pairs={{0,8},{4,12},{8,0},{12,4},{16,24},{20,28},{24,16},{28,20},{1,9},{5... | collective-permute-start | bytes 1597448 | tf_op jit(solution)/shard_map/ppermute | solution.py:98
  127.7 7.1 %collective-permute-start.16 = (f32[2,4,512]{2,1,0:T(4,128)S(1)}, f32[2,4,512]{2,1,0:T(4,128)S(1)}, u32[]{:S(2)}, u32[]{:S(2)}) collective-permute-start(f32[2,4,512]{2,1,0:T(4,128)S(1)} %get-tuple-element.36.weight.refs_4_), channel_id=1, source_target_pairs={{0,16},{4,20},{8,24},{12,28},{16,0},{20,4},{24,8},{28,12},{1,17},{... | collective-permute-start | bytes 49160 | tf_op jit(solution)/shard_map/ppermute | solution.py:98
  129.4 26.4 %collective-permute-start.18 = (f32[520,256]{1,0:T(8,128)S(1)}, f32[520,256]{1,0:T(8,128)S(1)}, u32[]{:S(2)}, u32[]{:S(2)}) collective-permute-start(f32[520,256]{1,0:T(8,128)S(1)} %collective-permute-done.11.refs_0_), channel_id=1, source_target_pairs={{0,2},{1,3},{2,0},{3,1},{4,6},{5,7},{6,4},{7,5},{8,10},{9,11},{10,... | collective-permute-start | bytes 1597448 | tf_op jit(solution)/shard_map/ppermute | solution.py:98
  129.9 26.0 %collective-permute-start.19 = (f32[520,256]{1,0:T(8,128)}, f32[520,256]{1,0:T(8,128)S(1)}, u32[]{:S(2)}, u32[]{:S(2)}) collective-permute-start(f32[520,256]{1,0:T(8,128)} %collective-permute-done.17.refs_1_), channel_id=1, source_target_pairs={{0,2},{1,3},{2,0},{3,1},{4,6},{5,7},{6,4},{7,5},{8,10},{9,11},{10,... | collective-permute-start | bytes 1597448 | tf_op jit(solution)/shard_map/ppermute | solution.py:98
  134.8 31.1 %collective-permute-start.13 = (f32[520,256]{1,0:T(8,128)}, f32[520,256]{1,0:T(8,128)S(1)}, u32[]{:S(2)}, u32[]{:S(2)}) collective-permute-start(f32[520,256]{1,0:T(8,128)} %collective-permute-done.12.refs_0_), channel_id=1, source_target_pairs={{0,1},{1,0},{2,3},{3,2},{4,5},{5,4},{6,7},{7,6},{8,9},{9,8},{10,11... | collective-permute-start | bytes 1597448 | tf_op jit(solution)/shard_map/ppermute | solution.py:98
  136.7 29.2 %collective-permute-start.15 = (f32[520,256]{1,0:T(8,128)}, f32[520,256]{1,0:T(8,128)S(1)}, u32[]{:S(2)}, u32[]{:S(2)}) collective-permute-start(f32[520,256]{1,0:T(8,128)} %collective-permute-done.14.refs_2_), channel_id=1, source_target_pairs={{0,1},{1,0},{2,3},{3,2},{4,5},{5,4},{6,7},{7,6},{8,9},{9,8},{10,11... | collective-permute-start | bytes 1597448 | tf_op jit(solution)/shard_map/ppermute | solution.py:98
  137.2 28.7 %collective-permute-start.9 = (f32[2,4,512]{2,1,0:T(4,128)S(1)}, f32[2,4,512]{2,1,0:T(4,128)S(1)}, u32[]{:S(2)}, u32[]{:S(2)}) collective-permute-start(f32[2,4,512]{2,1,0:T(4,128)S(1)} %get-tuple-element.36.weight.refs_4_), channel_id=1, source_target_pairs={{0,24},{4,28},{8,16},{12,20},{16,8},{20,12},{24,0},{28,4},{1,25},{... | collective-permute-start | bytes 49160 | tf_op jit(solution)/shard_map/ppermute | solution.py:98
  178.3 41.6 %collective-permute-start.24 = (f32[2560,256]{1,0:T(8,128)S(1)}, f32[2560,256]{1,0:T(8,128)S(1)}, u32[]{:S(2)}, u32[]{:S(2)}) collective-permute-start(f32[2560,256]{1,0:T(8,128)S(1)} %get-tuple-element.40), channel_id=1, source_target_pairs={{0,4},{4,0},{8,12},{12,8},{16,20},{20,16},{24,28},{28,24},{1,5},{5... | collective-permute-start | bytes 7864328 | tf_op jit(solution)/shard_map/ppermute | solution.py:98
  186.3 14.8 %collective-permute-start.6 = (f32[512,256]{1,0:T(8,128)S(1)}, f32[512,256]{1,0:T(8,128)S(1)}, u32[]{:S(2)}, u32[]{:S(2)}) collective-permute-start(f32[512,256]{1,0:T(8,128)S(1)} %get-tuple-element.33), channel_id=1, source_target_pairs={{0,1},{1,0},{2,3},{3,2},{4,5},{5,4},{6,7},{7,6},{8,9},{9,8},{10,11... | collective-permute-start | bytes 1572872 | tf_op jit(solution)/shard_map/ppermute | solution.py:98
  186.3 30.7 %collective-permute-start.7 = (f32[512,256]{1,0:T(8,128)S(1)}, f32[512,256]{1,0:T(8,128)S(1)}, u32[]{:S(2)}, u32[]{:S(2)}) collective-permute-start(f32[512,256]{1,0:T(8,128)S(1)} %get-tuple-element.34), channel_id=1, source_target_pairs={{0,2},{1,3},{2,0},{3,1},{4,6},{5,7},{6,4},{7,5},{8,10},{9,11},{10,... | collective-permute-start | bytes 1572872 | tf_op jit(solution)/shard_map/ppermute | solution.py:98
  194.1 24.9 %collective-permute-start.8 = (f32[512,256]{1,0:T(8,128)S(1)}, f32[512,256]{1,0:T(8,128)S(1)}, u32[]{:S(2)}, u32[]{:S(2)}) collective-permute-start(f32[512,256]{1,0:T(8,128)S(1)} %get-tuple-element.35), channel_id=1, source_target_pairs={{0,3},{1,2},{2,1},{3,0},{4,7},{5,6},{6,5},{7,4},{8,11},{9,10},{10,... | collective-permute-start | bytes 1572872 | tf_op jit(solution)/shard_map/ppermute | solution.py:98

commit v3 on v2

v3 whole, which is shorter than its diff:
```python
import functools

import jax
import jax.numpy as jnp
from jax import lax
from jax.experimental import pallas as pl
from jax.experimental.pallas import tpu as pltpu
from jax.sharding import PartitionSpec as P

TILE = 512
KMAX = 3
EXTRA = 8
STEP = 4
STAT = 4
MIB = 1024 * 1024
VMEM_LIMIT = 12 * MIB

very_low = -1e30
high, highest = lax.Precision.HIGH, lax.Precision.HIGHEST

smem = pl.BlockSpec(memory_space=pltpu.SMEM)
vmem = pl.BlockSpec(memory_space=pltpu.VMEM)
anywhere = pl.BlockSpec(memory_space=pl.ANY)
hbm = pl.BlockSpec(memory_space=pltpu.HBM)


def dot(a, b, dims=((1,), (0,)), precision=high):
    return lax.dot_general(a, b, (dims, ((), ())), precision=precision, preferred_element_type=jnp.float32)


def cost(us):
    return pl.CostEstimate(flops=0, bytes_accessed=int(us * 3.0e6), transcendentals=0)


def pack_kernel(step, ids_ref, counts_ref, q_ref, pos_ref, out_ref, sem):
    rows, width = q_ref.shape
    get_q = pltpu.make_async_copy(q_ref, out_ref.at[:rows], sem)
    get_q.start()
    out_ref[rows : rows + EXTRA, :] = jnp.zeros((EXTRA, width), jnp.float32)
    row = pos_ref[...].astype(jnp.float32)
    col = jnp.broadcast_to(row, (8, rows)).T[:, 0:1]
    at_row = lax.broadcasted_iota(jnp.int32, (rows, rows), 1)
    at_col = lax.broadcasted_iota(jnp.int32, (rows, rows), 0)
    before = (row < col) | ((row == col) & (at_row < at_col))
    rank = jnp.sum(before.astype(jnp.float32), axis=1, keepdims=True)
    placed = rank == at_row.astype(jnp.float32)
    sorted_pos = jnp.sum(jnp.where(placed, col, 0.0), axis=0, keepdims=True)
    sorted_at = jnp.sum(jnp.where(placed, at_col.astype(jnp.float32), 0.0), axis=0, keepdims=True)
    starts = lax.broadcasted_iota(jnp.int32, (rows, width), 1).astype(jnp.float32) * step
    bounds = jnp.sum((col < starts).astype(jnp.float32), axis=0, keepdims=True)
    lane = lax.broadcasted_iota(jnp.int32, (1, width), 1)
    lists = jnp.zeros((1, width), jnp.int32)
    n = counts_ref.shape[1]
    for i in range(n * KMAX):
        lists = jnp.where(lane == i, ids_ref[0, i // KMAX, i % KMAX], lists)
    for i in range(n):
        lists = jnp.where(lane == n * KMAX + i, counts_ref[0, i], lists)
    per = rows // width
    out_ref[rows + 3 * per : rows + 3 * per + 1, :] = lists.astype(jnp.float32)
    out_ref[rows + 3 * per + 1 : rows + 3 * per + 2, :] = bounds
    for first, values in ((0, row), (per, sorted_pos), (2 * per, sorted_at)):
        for i in range(per):
            out_ref[rows + first + i : rows + first + i + 1, :] = values[:, i * width : (i + 1) * width]
    get_q.wait()


def pack(queries, positive, tile_ids, counts, step):
    rows, width = queries.shape
    return pl.pallas_call(
        functools.partial(pack_kernel, float(step)),
        out_shape=jax.ShapeDtypeStruct((rows + EXTRA, width), jnp.float32),
        in_specs=[smem, smem, anywhere, vmem],
        out_specs=vmem,
        scratch_shapes=[pltpu.SemaphoreType.DMA],
        compiler_params=pltpu.CompilerParams(vmem_limit_bytes=VMEM_LIMIT),
        cost_estimate=cost(2),
        name="pack",
    )(tile_ids, counts, queries, positive.reshape(1, rows))


class Lists:
    def __init__(self, ref, rows, shard_at, n_shard):
        self.ref, self.rows, self.shard_at, self.n_shard = ref, rows, shard_at, n_shard
        self.width = ref.shape[2]
        self.per = rows // self.width
        self.shift = self.width.bit_length() - 1

    def entry(self, b, first, i):
        return self.ref[b, first + (i >> self.shift), i & (self.width - 1)]

    def sorted_pos(self, b, i):
        return self.entry(b, self.per, i)

    def place(self, b, i):
        return self.entry(b, 2 * self.per, i)

    def tile(self, b, k):
        return self.ref[b, 3 * self.per, self.shard_at * KMAX + k]

    def count(self, b):
        return self.ref[b, 3 * self.per, self.n_shard * KMAX + self.shard_at]

    def bound(self, b, i):
        return self.ref[b, 3 * self.per + 1, i]


def swap(x, axis, bits):
    return lax.ppermute(x, axis, [(i, i ^ bits) for i in range(lax.axis_size(axis))])


def together(*xs):
    return lax.optimization_barrier(xs)


def stats_kernel(n, n_before, n_shard, at, *refs):
    msgs, refs = refs[:n], refs[n:]
    befores, refs = refs[:n_before], refs[n_before:]
    items_hbm, acc_ref, chosen_ref, stat_ref, q_ref, tiles, rowbuf, whole, lists_ref, sems, row_sems = refs
    rows = q_ref.shape[1] - EXTRA
    width = q_ref.shape[2]
    per = rows // width
    lists = Lists(lists_ref, rows, at[0], n_shard)
    base, local_rows = at[1], items_hbm.shape[0]
    get_lists = pltpu.make_async_copy(whole, lists_ref, sems.at[1, 0])

    def get_q(j):
        return pltpu.make_async_copy(msgs[j], q_ref.at[j], sems.at[0, j])

    def get_tile(b, k):
        start = pl.multiple_of(lists.tile(b, k) * TILE, TILE)
        return pltpu.make_async_copy(items_hbm.at[pl.ds(start, TILE)], tiles.at[b * KMAX + k], sems.at[2 + k, b])

    def get_row(b, i):
        return pltpu.make_async_copy(
            items_hbm.at[pl.ds(lists.sorted_pos(b, i) - base, 1)], rowbuf.at[b, pl.ds(lists.place(b, i), 1)], row_sems.at[b]
        )

    def row_loop(b):
        return pl.loop(lists.bound(b, at[0] * at[4]), lists.bound(b, (at[0] + 1) * at[4]))

    for j in range(n):
        get_q(j).start()
    rowbuf[...] = jnp.zeros(rowbuf.shape, jnp.float32)
    first = 0
    for before in befores:
        stat_ref[first : first + before.shape[0]] = before[...]
        first += before.shape[0]
    for j in range(n):
        get_q(j).wait()
    whole[...] = q_ref[:, rows:, :].astype(jnp.int32)
    get_lists.start()
    get_lists.wait()

    @pl.loop(0, n)
    def _(b):
        @pl.loop(0, lists.count(b))
        def _(k):
            get_tile(b, k).start()

    @pl.loop(0, n)
    def _(b):
        @row_loop(b)
        def _(i):
            get_row(b, i).start()

    @pl.loop(0, n)
    def _(b):
        q_t = q_ref[b, :rows, :].T
        acc_ref[b] = jnp.zeros(acc_ref.shape[1:], jnp.float32)

        def visit(k, carry):
            top, total = carry
            get_tile(b, k).wait()
            tile = tiles[b * KMAX + k]
            logits = dot(tile, q_t, precision=highest)
            new_top = jnp.maximum(top, jnp.max(logits, axis=0, keepdims=True))
            prob = jnp.exp(logits - new_top)
            scale = jnp.exp(top - new_top)
            total = total * scale + jnp.sum(prob, axis=0, keepdims=True)
            acc_ref[b] = acc_ref[b] * scale + dot(tile.T, prob)
            return new_top, total

        start = (jnp.full((1, rows), very_low, jnp.float32), jnp.zeros((1, rows), jnp.float32))
        top, total = lax.fori_loop(0, lists.count(b), visit, start)

        @row_loop(b)
        def _(i):
            get_row(b, i).wait()

        chosen = rowbuf[b].T
        chosen_ref[b] = chosen
        pos = jnp.concatenate([q_ref[b, rows + i : rows + i + 1, :] for i in range(per)], axis=1).astype(jnp.int32)
        offset = pos - base
        inside = (offset >= 0) & (offset < local_rows)
        plogit = jnp.sum(q_t * chosen, axis=0, keepdims=True)
        new_top = jnp.maximum(top, jnp.where(inside, plogit, very_low))
        total = total * jnp.exp(top - new_top) + jnp.where(inside, jnp.exp(plogit - new_top), 0.0)
        stat_ref[first + b, 0:1, :] = top
        stat_ref[first + b, 1:2, :] = new_top + jnp.log(total)
        stat_ref[first + b, 2:3, :] = jnp.where(inside, plogit, 0.0)
        stat_ref[first + b, 3:4, :] = jnp.where(inside, 1.0, 0.0)


def stats(messages, befores, items, at):
    n = len(messages)
    rows, width = messages[0].shape[0] - EXTRA, messages[0].shape[1]
    total = n + sum(b.shape[0] for b in befores)
    sums = jax.ShapeDtypeStruct((n, width, rows), jnp.float32)
    return pl.pallas_call(
        functools.partial(stats_kernel, n, len(befores), lax.axis_size("shard")),
        out_shape=(sums, sums, jax.ShapeDtypeStruct((total, STAT, rows), jnp.float32)),
        in_specs=[smem] + [anywhere] * n + [vmem] * len(befores) + [hbm],
        out_specs=(vmem, vmem, vmem),
        scratch_shapes=[
            pltpu.VMEM((n, rows + EXTRA, width), jnp.float32),
            pltpu.VMEM((n * KMAX, TILE, width), jnp.float32),
            pltpu.VMEM((n, rows, width), jnp.float32),
            pltpu.VMEM((n, EXTRA, width), jnp.int32),
            pltpu.SMEM((n, EXTRA, width), jnp.int32),
            pltpu.SemaphoreType.DMA((2 + KMAX, n)),
            pltpu.SemaphoreType.DMA((n,)),
        ],
        compiler_params=pltpu.CompilerParams(vmem_limit_bytes=VMEM_LIMIT + n * 3 * MIB),
        cost_estimate=cost(5 * n),
        name="stats",
    )(at, *messages, *befores, items)


def dq_kernel(n, counts, *refs):
    stat_refs, refs = refs[:n], refs[n:]
    acc_refs, refs = refs[: len(counts)], refs[len(counts) :]
    chosen_refs, refs = refs[: len(counts)], refs[len(counts) :]
    loss_ref, term_ref, share_refs = refs[0], refs[1], refs[2:]
    b = 0
    for acc_ref, chosen_ref, count in zip(acc_refs, chosen_refs, counts):
        for i in range(count):
            parts = [stat_refs[j][b ^ j, 1:2, :] for j in range(n)]
            top = functools.reduce(jnp.maximum, parts)
            lse = top + jnp.log(sum(jnp.exp(p - top) for p in parts))
            plogit = sum(stat_refs[j][b ^ j, 2:3, :] for j in range(n))
            weight = jnp.exp(plogit - lse) - 1.0
            term_ref[0, b : b + 1, :] = lse
            term_ref[1, b : b + 1, :] = weight
            if b == 0:
                loss_ref[...] = lse - plogit
            own = stat_refs[0]
            share = acc_ref[i] * jnp.exp(own[b, 0:1, :] - lse) + chosen_ref[i] * (weight * own[b, 3:4, :])
            share_refs[b][...] = share.T
            b += 1


def dq_shares(all_stats, accs, chosens):
    n, _, rows = all_stats[0].shape
    width = accs[0].shape[1]
    share = jax.ShapeDtypeStruct((rows, width), jnp.float32)
    loss, terms, *shares = pl.pallas_call(
        functools.partial(dq_kernel, n, [a.shape[0] for a in accs]),
        out_shape=(jax.ShapeDtypeStruct((1, rows), jnp.float32), jax.ShapeDtypeStruct((2, n, rows), jnp.float32), *[share] * n),
        compiler_params=pltpu.CompilerParams(vmem_limit_bytes=VMEM_LIMIT),
        cost_estimate=cost(3),
        name="dq",
    )(*all_stats, *accs, *chosens)
    return loss, terms, shares


def item_kernel(n, n_shard, n_waits, is_first, is_last, at, weight, *refs):
    msgs, refs = refs[:n], refs[n + n_waits :]
    lse_ref, items, refs = refs[0], refs[1], refs[2 if is_first else 3 :]
    acc, token, refs = refs[0], refs[1], refs[2:]
    if is_first:
        source, items, refs = items, refs[0], refs[1:]
    outs, refs = refs[: 2 * is_last], refs[2 * is_last :]
    q_ref, whole, lists_ref, sems = refs
    rows, width = q_ref.shape[1] - EXTRA, q_ref.shape[2]
    span_rows = acc.shape[0]
    tiles = span_rows // TILE
    base, first_tile, core = at[1] + at[2] * TILE, at[2], at[3]
    chip = at[0] * at[4] + at[5]
    lists = Lists(lists_ref, rows, at[0], n_shard)
    get_lists = pltpu.make_async_copy(whole, lists_ref, sems.at[1, 0])

    def get_q(j):
        return pltpu.make_async_copy(msgs[j], q_ref.at[j], sems.at[0, j])

    for j in range(n):
        get_q(j).start()
    if is_first:
        start = pl.multiple_of(first_tile * TILE, TILE)
        get_items = pltpu.make_async_copy(source.at[pl.ds(start, span_rows)], items, sems.at[2, 0])
        get_items.start()
        acc[...] = jnp.zeros(acc.shape, jnp.float32)
    token[...] = jnp.zeros(token.shape, jnp.float32)
    for j in range(n):
        get_q(j).wait()
    whole[...] = q_ref[:, rows:, :].astype(jnp.int32)
    get_lists.start()
    get_lists.wait()

    @pl.loop(0, n)
    def _(b):
        low, top = lists.bound(b, chip), lists.bound(b, chip + 1)

        @pl.loop(0, (top - low + STEP - 1) // STEP)
        def _(c):
            entries = [jnp.minimum(low + c * STEP + u, top - 1) for u in range(STEP)]
            rests = [jnp.where(low + c * STEP + u < top, 1.0, 0.0) for u in range(STEP)]
            heres = [lists.sorted_pos(b, i) - base for i in entries]
            places = [lists.place(b, i) for i in entries]
            olds = [acc[pl.ds(h, 1), :] for h in heres]
            terms = [q_ref[b, pl.ds(p, 1), :] * (weight[1, b, p] * r) for p, r in zip(places, rests)]
            for u in range(1, STEP):
                terms[u] = terms[u] + terms[u - 1] * jnp.where(heres[u] == heres[u - 1], 1.0, 0.0)
            for h, old, term in zip(heres, olds, terms):
                acc[pl.ds(h, 1), :] = old + term

    if is_first:
        get_items.wait()

    @pl.loop(0, n)
    def _(b):
        @pl.loop(0, lists.count(b))
        def _(k):
            tile = lists.tile(b, k) - first_tile

            @pl.when((tile >= 0) & (tile < tiles))
            def _():
                here = pl.ds(pl.multiple_of(tile * TILE, TILE), TILE)
                q = q_ref[b, :rows, :]
                logits = dot(items[here, :], q, ((1,), (1,)), highest)
                prob = jnp.exp(logits - lse_ref[0, pl.ds(b, 1), :])
                acc[here, :] += dot(prob, q)

    if is_last:
        own = span_rows // 2
        mine, other = outs
        put = [
            pltpu.make_async_copy(acc.at[pl.ds(pl.multiple_of((1 - core) * own, 8), own)], other, sems.at[2, 0]),
            pltpu.make_async_copy(acc.at[pl.ds(pl.multiple_of(core * own, 8), own)], mine, sems.at[2, 1]),
        ]
        for p in put:
            p.start()
        for p in put:
            p.wait()


def item_grads(messages, terms, items, acc, span_rows, at, is_last, waits=()):
    n = len(messages)
    rows, width = messages[0].shape[0] - EXTRA, messages[0].shape[1]
    is_first = acc is None
    half = jax.ShapeDtypeStruct((span_rows // 2, width), jnp.float32)
    chips = pltpu.VMEM((span_rows, width), jnp.float32)
    token = jax.ShapeDtypeStruct((1, 128), jnp.float32)
    more = [chips] if is_first else [half, half] if is_last else []
    carried = [] if is_first else [acc]
    return pl.pallas_call(
        functools.partial(item_kernel, n, lax.axis_size("shard"), len(waits), is_first, is_last),
        out_shape=(chips, token, *more),
        in_specs=[smem] * 2 + [anywhere] * (n + len(waits)) + [vmem, hbm if is_first else vmem] + [vmem] * len(carried),
        out_specs=(vmem, vmem, *[vmem if is_first else anywhere] * len(more)),
        scratch_shapes=[
            pltpu.VMEM((n, rows + EXTRA, width), jnp.float32),
            pltpu.VMEM((n, EXTRA, width), jnp.int32),
            pltpu.SMEM((n, EXTRA, width), jnp.int32),
            pltpu.SemaphoreType.DMA((3, max(n, 2))),
        ],
        input_output_aliases={} if is_first else {4 + n + len(waits): 0},
        compiler_params=pltpu.CompilerParams(vmem_limit_bytes=VMEM_LIMIT),
        cost_estimate=cost(2 * n),
        name="item_grads",
    )(at, terms, *messages, *waits, terms, items, *carried)


def local(queries, items, positive, tile_ids, counts):
    dp_at, shard_at = lax.axis_index("dp"), lax.axis_index("shard")
    n_dp, n_shard = lax.axis_size("dp"), lax.axis_size("shard")
    rows, width = queries.shape
    local_rows = items.shape[0]
    span_rows = 2 * (local_rows // n_dp)
    n_chips = n_dp // 2
    chip_at = dp_at // 2
    at = jnp.stack([shard_at, shard_at * local_rows, chip_at * (span_rows // TILE), dp_at % 2, n_chips, chip_at])
    at = at.astype(jnp.int32)

    def top(j):
        return 1 << (j.bit_length() - 1)

    items = pltpu.with_memory_space_constraint(items, pltpu.HBM)
    message = pack(queries, positive, tile_ids, counts, span_rows)
    own = [message] + [swap(message, "shard", j) for j in (1, 2)]
    straight = [message] + [swap(message, "dp", 2 * k) for k in range(1, n_chips)]
    acc0, chosen0, stat0 = stats([message], [], items, at)
    own[1], own[2], stat0 = together(own[1], own[2], stat0)
    for j in range(3, n_shard):
        own.append(swap(own[j ^ top(j)], "shard", top(j)))
    near = [straight[1], swap(own[1], "dp", 2)]
    acc1, chosen1, stat1 = stats(own[1:3], [stat0], items, at)
    straight[1], straight[2], stat1, *own[3:] = together(straight[1], straight[2], stat1, *own[3:])
    near[0] = straight[1]
    far = {2: [straight[2]] + [swap(straight[2], "shard", j) for j in (1, 2)]}
    acc2, chosen2, stat = stats(own[3:], [stat1], items, at)

    all_stats = [stat]
    bit = 1
    while bit < n_shard:
        got = swap(jnp.stack(all_stats) if bit > 1 else stat, "shard", bit)
        all_stats += [got[j] for j in range(bit)] if bit > 1 else [got]
        bit *= 2
    all_stats[0], near[1], far[2][1], far[2][2], *straight[3:] = together(
        all_stats[0], near[1], far[2][1], far[2][2], *straight[3:]
    )
    loss, sent, shares = dq_shares(all_stats, [acc0, acc1, acc2], [chosen0, chosen1, chosen2])
    for j in range(3, n_shard):
        far[2].append(swap(far[2][j ^ top(j)], "shard", top(j)))

    grads, token, chip_items = item_grads(own, sent, items, None, span_rows, at, False)
    terms = [sent]
    bit = 1
    while bit < n_chips:
        got = swap(jnp.stack(terms) + token[0, 0] if bit > 1 else sent, "dp", 2 * bit)
        terms += [got[j] for j in range(bit)] if bit > 1 else [got]
        bit *= 2
    for k in range(3, n_chips):
        far[k] = [straight[k]] + [swap(straight[k], "shard", j) for j in (1, 2)]
    rest = jnp.concatenate(own[2:]) + jnp.minimum(jnp.abs(terms[n_chips - 1][0, 0, 0]), 0.0)
    rest = swap(rest, "dp", 2)
    size = rows + EXTRA
    near += [rest[i * size : (i + 1) * size] for i in range(n_shard - 2)]
    grads = item_grads(far[2], terms[2], chip_items, grads, span_rows, at, False)[0]

    for k in range(3, n_chips):
        for j in range(3, n_shard):
            far[k].append(swap(far[k][j ^ top(j)], "shard", top(j)))
    sums = dict(enumerate(shares))
    bit = 1
    while bit < n_shard:
        sums = {j: sums[j] + swap(sums[j ^ bit], "shard", bit) for j in sorted(sums, reverse=True) if not j & bit}
        bit *= 2
    query_grad = sums[0]
    grads = item_grads(near, terms[1], chip_items, grads, span_rows, at, False)[0]
    for k in range(3, n_chips):
        is_last = k == n_chips - 1
        out = item_grads(far[k], terms[k], chip_items, grads, span_rows, at, is_last, [query_grad] if is_last else [])
        grads = out[0]
    mine, other = out[2:]
    item_grad = mine + swap(other, "dp", 1)
    return loss.reshape(rows), query_grad, item_grad


def solution(mesh):
    placed = (
        P(("dp", "shard"), None),
        P("shard", None),
        P(("dp", "shard")),
        P(("dp", "shard"), None, None),
        P(("dp", "shard"), None),
    )
    return jax.shard_map(
        local,
        mesh=mesh,
        in_specs=placed,
        out_specs=(P(("dp", "shard")), P(("dp", "shard"), None), P(("shard", "dp"), None)),
        check_vma=False,
    )
```

time: 221 us -> 148 us (0.67)
  the two profiles are of different devices: /device:TPU:0 before, /device:TPU:21 now
where the time goes in v3:
time: 148 us
  Pallas kernels  69.7 us (47%)
  starting transfers between devices  35.5 us (24%)
  waiting for transfers between devices  35.3 us (24%)
  local copies, waits for them, and re-layouts  3.83 us (3%)
  other arithmetic  2.13 us (1%)
  between operations  1.5 us (1%)
    pallas_call x4, Pallas kernels, item_grads(): pl.pallas_call(functools.partial(item_kernel, n, lax.axis_size('shard'),...  35.5 us
    ppermute x22, starting transfers between devices, swap(): lax.ppermute(x, axis, [(i, i ^ bits) for i in range(lax.axis_size(axis))])  35.5 us
    ppermute x22, waiting for transfers between devices, swap(): lax.ppermute(x, axis, [(i, i ^ bits) for i in range(lax.axis_size(axis))])  35.3 us
    pallas_call x3, Pallas kernels, stats(): pl.pallas_call(functools.partial(stats_kernel, n, len(befores), lax.axis_...  31.9 us
    unnamed x9, local copies, waits for them, and re-layouts  3.15 us
  transfers between devices with their start and end apart: 22, of which 9 were waited for; matrix products, arithmetic and copies ran while one was open for 1% of the time, Pallas kernels for 39%

profile of v3, /device:TPU:21, one launch (start us, length us, event | category | flops | bytes accessed | tf_op | source)
XLA Modules:
  0.0 147.9 jit_solution(11473318910095299944)
XLA Ops:
  1.4 1.0 copy-done.1
  3.8 1.2 pack.1.refs_0_
  5.3 1.2 collective-permute-start.2
  6.5 1.3 collective-permute-start
  7.9 6.5 %stats.3 = (f32[1,256,512]{2,1,0:T(8,128)S(1)}, f32[1,256,512]{2,1,0:T(8,128)S(1)}, f32[1,4,512]{2,1,0:T(4,128)S(1)}) custom-call(s32[6]{0:T(128)S(1)} %stack.41.at, f32[520,256]{1,0:T(8,128)S(1)} %pack.1.refs_0_, f32[20480,256]{1,0:T(8,128)} %refs_5_.1), custom_call_target="tpu_custom_call" | custom-call | bytes 15000000 | tf_op jit(solution)/shard_map/stats/pallas_call | solution.py:209
  14.5 3.6 %collective-permute-done.3.refs_1_.refs_2_ = f32[520,256]{1,0:T(8,128)S(1)} collective-permute-done((f32[520,256]{1,0:T(8,128)S(1)}, f32[520,256]{1,0:T(8,128)S(1)}, u32[]{:S(2)}, u32[]{:S(2)}) %collective-permute-start.3) | collective-permute-done | bytes 532512 | tf_op jit(solution)/shard_map/ppermute | solution.py:108
  18.0 1.1 collective-permute-start.4
  19.3 1.1 collective-permute-start.5
  20.5 16.7 %stats.4 = (f32[2,256,512]{2,1,0:T(8,128)S(1)}, f32[2,256,512]{2,1,0:T(8,128)S(1)}, f32[3,4,512]{2,1,0:T(4,128)S(1)}) custom-call(s32[6]{0:T(128)S(1)} %stack.41.at, f32[520,256]{1,0:T(8,128)S(1)} %collective-permute-done.2.refs_0_.refs_1_, f32[520,256]{1,0:T(8,128)S(1)} %collective-permute-done.3.refs_1_.refs_2_, ...), custom_call_target="tpu_custom_call" | custom-call | bytes 30000000 | tf_op jit(solution)/shard_map/stats/pallas_call | solution.py:209
  37.6 4.3 %collective-permute-start.6 = (f32[520,256]{1,0:T(8,128)S(1)}, f32[520,256]{1,0:T(8,128)S(1)}, u32[]{:S(2)}, u32[]{:S(2)}) collective-permute-start(f32[520,256]{1,0:T(8,128)S(1)} %collective-permute-done.1.refs_0_), channel_id=1, source_target_pairs={{0,1},{1,0},{2,3},{3,2},{4,5},{5,4},{6,7},{7,6},{8,9},{9,8},{10,11... | collective-permute-start | bytes 1597448 | tf_op jit(solution)/shard_map/ppermute | solution.py:108
  41.9 8.6 %stats.5 = (f32[1,256,512]{2,1,0:T(8,128)S(1)}, f32[1,256,512]{2,1,0:T(8,128)S(1)}, f32[4,4,512]{2,1,0:T(4,128)S(1)}) custom-call(s32[6]{0:T(128)S(1)} %stack.41.at, f32[520,256]{1,0:T(8,128)S(1)} %collective-permute-done.4.refs_0_.refs_3_, f32[3,4,512]{2,1,0:T(4,128)S(1)} %get-tuple-element.43.refs_1_, f32[20480,256]{1,0:T(8,128)} %refs_5_.1), custom_call_target="tpu_custom_call" | custom-call | bytes 15000000 | tf_op jit(solution)/shard_map/stats/pallas_call | solution.py:209
  50.5 1.7 %collective-permute-start.9 = (f32[4,4,512]{2,1,0:T(4,128)S(1)}, f32[4,4,512]{2,1,0:T(4,128)S(1)}, u32[]{:S(2)}, u32[]{:S(2)}) collective-permute-start(f32[4,4,512]{2,1,0:T(4,128)S(1)} %get-tuple-element.46.refs_0_), channel_id=1, source_target_pairs={{0,1},{1,0},{2,3},{3,2},{4,5},{5,4},{6,7},{7,6},{8,9},{9,8},{10,11... | collective-permute-start | bytes 98312 | tf_op jit(solution)/shard_map/ppermute | solution.py:108
  52.2 2.0 %collective-permute-done.9.refs_1_ = f32[4,4,512]{2,1,0:T(4,128)S(1)} collective-permute-done((f32[4,4,512]{2,1,0:T(4,128)S(1)}, f32[4,4,512]{2,1,0:T(4,128)S(1)}, u32[]{:S(2)}, u32[]{:S(2)}) %collective-permute-start.9) | collective-permute-done | bytes 32800 | tf_op jit(solution)/shard_map/ppermute | solution.py:108
  54.3 1.1 collective-permute-start.10
  55.4 2.0 %collective-permute-done.10 = f32[2,4,4,512]{3,2,1,0:T(4,128)S(1)} collective-permute-done((f32[2,4,4,512]{3,2,1,0:T(4,128)S(1)}, f32[2,4,4,512]{3,2,1,0:T(4,128)S(1)}, u32[]{:S(2)}, u32[]{:S(2)}) %collective-permute-start.10) | collective-permute-done | bytes 65568 | tf_op jit(solution)/shard_map/ppermute | solution.py:108
  57.5 1.2 dq.1
  58.7 7.2 %item_grads.4 = (f32[5120,256]{1,0:T(8,128)S(1)}, f32[1,128]{1,0:T(1,128)S(1)}, f32[5120,256]{1,0:T(8,128)S(1)}) custom-call(s32[6]{0:T(128)S(1)} %stack.41.at, f32[2,4,512]{2,1,0:T(4,128)S(1)} %get-tuple-element.58.weight.refs_4_, f32[520,256]{1,0:T(8,128)S(1)} %pack.1.refs_0_, f32[520,256]{1,0:T(8,128)S(1)} %collective-permute-done.2.refs_0_.refs_1_, ...), custom_call_target="tpu_custom_call" | custom-call | bytes 24000000 | tf_op jit(solution)/shard_map/item_grads/pallas_call | solution.py:355
  65.9 5.2 %collective-permute-start.15 = (f32[2,2,4,512]{3,2,1,0:T(4,128)S(1)}, f32[2,2,4,512]{3,2,1,0:T(4,128)S(1)}, u32[]{:S(2)}, u32[]{:S(2)}) collective-permute-start(f32[2,2,4,512]{3,2,1,0:T(4,128)S(1)} %maximum_add_fusion.1), channel_id=1, source_target_pairs={{0,16},{4,20},{8,24},{12,28},{16,0},{20,4},{24,8},{28,12},{1,17},{... | collective-permute-start | bytes 98312 | tf_op jit(solution)/shard_map/ppermute | solution.py:108
  71.1 1.3 collective-permute-done.15
  73.7 4.0 %collective-permute-start.19 = (f32[1040,256]{1,0:T(8,128)S(1)}, f32[1040,256]{1,0:T(8,128)S(1)}, u32[]{:S(2)}, u32[]{:S(2)}) collective-permute-start(f32[1040,256]{1,0:T(8,128)S(1)} %maximum_add_fusion), channel_id=1, source_target_pairs={{0,8},{4,12},{8,0},{12,4},{16,24},{20,28},{24,16},{28,20},{1,9},{5... | collective-permute-start | bytes 3194888 | tf_op jit(solution)/shard_map/ppermute | solution.py:108
  77.7 3.3 %collective-permute-start.20 = (f32[520,256]{1,0:T(8,128)S(1)}, f32[520,256]{1,0:T(8,128)S(1)}, u32[]{:S(2)}, u32[]{:S(2)}) collective-permute-start(f32[520,256]{1,0:T(8,128)S(1)} %collective-permute-done.6.refs_1_), channel_id=1, source_target_pairs={{0,2},{1,3},{2,0},{3,1},{4,6},{5,7},{6,4},{7,5},{8,10},{9,11},{10,... | collective-permute-start | bytes 1597448 | tf_op jit(solution)/shard_map/ppermute | solution.py:108
  81.0 1.5 collective-permute-start.11
  82.6 8.7 %collective-permute-done.20.refs_3_ = f32[520,256]{1,0:T(8,128)S(1)} collective-permute-done((f32[520,256]{1,0:T(8,128)S(1)}, f32[520,256]{1,0:T(8,128)S(1)}, u32[]{:S(2)}, u32[]{:S(2)}) %collective-permute-start.20) | collective-permute-done | bytes 532512 | tf_op jit(solution)/shard_map/ppermute | solution.py:108
  91.4 2.2 %collective-permute-start.17 = (f32[520,256]{1,0:T(8,128)S(1)}, f32[520,256]{1,0:T(8,128)S(1)}, u32[]{:S(2)}, u32[]{:S(2)}) collective-permute-start(f32[520,256]{1,0:T(8,128)S(1)} %collective-permute-done.8.refs_0_), channel_id=1, source_target_pairs={{0,2},{1,3},{2,0},{3,1},{4,6},{5,7},{6,4},{7,5},{8,10},{9,11},{10,... | collective-permute-start | bytes 1597448 | tf_op jit(solution)/shard_map/ppermute | solution.py:108
  93.6 1.6 %collective-permute-done.16.refs_1_ = f32[520,256]{1,0:T(8,128)S(1)} collective-permute-done((f32[520,256]{1,0:T(8,128)S(1)}, f32[520,256]{1,0:T(8,128)S(1)}, u32[]{:S(2)}, u32[]{:S(2)}) %collective-permute-start.16) | collective-permute-done | bytes 532512 | tf_op jit(solution)/shard_map/ppermute | solution.py:108
  95.2 11.0 %item_grads.5 = (f32[5120,256]{1,0:T(8,128)S(1)}, f32[1,128]{1,0:T(1,128)}) custom-call(s32[6]{0:T(128)S(1)} %stack.41.at, f32[2,4,512]{2,1,0:T(4,128)S(1)} %get-tuple-element.75.weight.refs_4_, f32[520,256]{1,0:T(8,128)S(1)} %collective-permute-done.1.refs_0_, f32[520,256]{1,0:T(8,128)S(1)} %collective-permute-done.6.refs_1_, ...), custom_call_target="tpu_custom_call", output_to_operand_aliasing={{0}: (8, {})} | custom-call | bytes 24000000 | tf_op jit(solution)/shard_map/item_grads/pallas_call | solution.py:355
  106.6 7.6 %item_grads.6 = (f32[5120,256]{1,0:T(8,128)S(1)}, f32[1,128]{1,0:T(1,128)}) custom-call(s32[6]{0:T(128)S(1)} %stack.41.at, f32[2,4,512]{2,1,0:T(4,128)S(1)} %collective-permute-done.14.weight.refs_4_, f32[520,256]{1,0:T(8,128)S(1)} %collective-permute-done.refs_0_, f32[520,256]{1,0:T(8,128)S(1)} %collective-permute-done.5.refs_1_, ...), custom_call_target="tpu_custom_call", output_to_operand_aliasing={{0}: (8, {})} | custom-call | bytes 24000000 | tf_op jit(solution)/shard_map/item_grads/pallas_call | solution.py:355
  114.3 11.1 %collective-permute-done.18.refs_3_ = f32[520,256]{1,0:T(8,128)S(1)} collective-permute-done((f32[520,256]{1,0:T(8,128)S(1)}, f32[520,256]{1,0:T(8,128)S(1)}, u32[]{:S(2)}, u32[]{:S(2)}) %collective-permute-start.18) | collective-permute-done | bytes 532512 | tf_op jit(solution)/shard_map/ppermute | solution.py:108
  125.4 9.7 %item_grads.7 = (f32[5120,256]{1,0:T(8,128)S(1)}, f32[1,128]{1,0:T(1,128)}, f32[2560,256]{1,0:T(8,128)S(1)}, f32[2560,256]{1,0:T(8,128)S(1)}) custom-call(s32[6]{0:T(128)S(1)} %stack.41.at, f32[2,4,512]{2,1,0:T(4,128)S(1)} %get-tuple-element.76.weight.refs_5_, f32[520,256]{1,0:T(8,128)S(1)} %collective-permute-done.8.refs_0_, ...), custom_call_target="tpu_custom_call", output_to_operand_aliasing={{0}: (9, {})} | custom-call | bytes 24000000 | tf_op jit(solution)/shard_map/item_grads/pallas_call | solution.py:355
  135.1 6.4 %collective-permute-start.21 = (f32[2560,256]{1,0:T(8,128)S(1)}, f32[2560,256]{1,0:T(8,128)S(1)}, u32[]{:S(2)}, u32[]{:S(2)}) collective-permute-start(f32[2560,256]{1,0:T(8,128)S(1)} %get-tuple-element.70), channel_id=1, source_target_pairs={{0,4},{4,0},{8,12},{12,8},{16,20},{20,16},{24,28},{28,24},{1,5},{5... | collective-permute-start | bytes 7864328 | tf_op jit(solution)/shard_map/ppermute | solution.py:108
  141.6 4.5 %collective-permute-done.21 = f32[2560,256]{1,0:T(8,128)S(1)} collective-permute-done((f32[2560,256]{1,0:T(8,128)S(1)}, f32[2560,256]{1,0:T(8,128)S(1)}, u32[]{:S(2)}, u32[]{:S(2)}) %collective-permute-start.21) | collective-permute-done | bytes 2621472 | tf_op jit(solution)/shard_map/ppermute | solution.py:108
  146.1 1.8 %add.37 = f32[2560,256]{1,0:T(8,128)} add(f32[2560,256]{1,0:T(8,128)S(1)} %get-tuple-element.69, f32[2560,256]{1,0:T(8,128)S(1)} %collective-permute-done.21) | non-fusion elementwise | flops 655360 | bytes 7864320 | tf_op jit(solution)/shard_map/add | solution.py:445
  (41 shorter events, 4.4 us)
Async XLA Ops:
  1.4 1.0 copy-start.1
  2.4 0.7 copy-start.2
  3.1 0.7 copy-start.3
  5.0 13.0 %collective-permute-start.3 = (f32[520,256]{1,0:T(8,128)S(1)}, f32[520,256]{1,0:T(8,128)S(1)}, u32[]{:S(2)}, u32[]{:S(2)}) collective-permute-start(f32[520,256]{1,0:T(8,128)S(1)} %pack.1.refs_0_), channel_id=1, source_target_pairs={{0,2},{1,3},{2,0},{3,1},{4,6},{5,7},{6,4},{7,5},{8,10},{9,11},{10,... | collective-permute-start | bytes 1597448 | tf_op jit(solution)/shard_map/ppermute | solution.py:108
  5.3 12.7 %collective-permute-start.2 = (f32[520,256]{1,0:T(8,128)S(1)}, f32[520,256]{1,0:T(8,128)S(1)}, u32[]{:S(2)}, u32[]{:S(2)}) collective-permute-start(f32[520,256]{1,0:T(8,128)S(1)} %pack.1.refs_0_), channel_id=1, source_target_pairs={{0,1},{1,0},{2,3},{3,2},{4,5},{5,4},{6,7},{7,6},{8,9},{9,8},{10,11... | collective-permute-start | bytes 1597448 | tf_op jit(solution)/shard_map/ppermute | solution.py:108
  6.5 30.7 %collective-permute-start.1 = (f32[520,256]{1,0:T(8,128)S(1)}, f32[520,256]{1,0:T(8,128)S(1)}, u32[]{:S(2)}, u32[]{:S(2)}) collective-permute-start(f32[520,256]{1,0:T(8,128)S(1)} %pack.1.refs_0_), channel_id=1, source_target_pairs={{0,16},{4,20},{8,24},{12,28},{16,0},{20,4},{24,8},{28,12},{1,17},{... | collective-permute-start | bytes 1597448 | tf_op jit(solution)/shard_map/ppermute | solution.py:108
  6.5 30.7 %collective-permute-start = (f32[520,256]{1,0:T(8,128)S(1)}, f32[520,256]{1,0:T(8,128)S(1)}, u32[]{:S(2)}, u32[]{:S(2)}) collective-permute-start(f32[520,256]{1,0:T(8,128)S(1)} %pack.1.refs_0_), channel_id=1, source_target_pairs={{0,8},{4,12},{8,0},{12,4},{16,24},{20,28},{24,16},{28,20},{1,9},{5... | collective-permute-start | bytes 1597448 | tf_op jit(solution)/shard_map/ppermute | solution.py:108
  18.0 19.2 %collective-permute-start.4 = (f32[520,256]{1,0:T(8,128)S(1)}, f32[520,256]{1,0:T(8,128)S(1)}, u32[]{:S(2)}, u32[]{:S(2)}) collective-permute-start(f32[520,256]{1,0:T(8,128)S(1)} %collective-permute-done.2.refs_0_.refs_1_), channel_id=1, source_target_pairs={{0,2},{1,3},{2,0},{3,1},{4,6},{5,7},{6,4},{7,5},{8,10},{9,11},{10,... | collective-permute-start | bytes 1597448 | tf_op jit(solution)/shard_map/ppermute | solution.py:108
  19.2 38.3 %collective-permute-start.8 = (f32[520,256]{1,0:T(8,128)S(1)}, f32[520,256]{1,0:T(8,128)S(1)}, u32[]{:S(2)}, u32[]{:S(2)}) collective-permute-start(f32[520,256]{1,0:T(8,128)S(1)} %pack.1.refs_0_), channel_id=1, source_target_pairs={{0,24},{4,28},{8,16},{12,20},{16,8},{20,12},{24,0},{28,4},{1,25},{... | collective-permute-start | bytes 1597448 | tf_op jit(solution)/shard_map/ppermute | solution.py:108
  19.3 38.1 %collective-permute-start.5 = (f32[520,256]{1,0:T(8,128)S(1)}, f32[520,256]{1,0:T(8,128)S(1)}, u32[]{:S(2)}, u32[]{:S(2)}) collective-permute-start(f32[520,256]{1,0:T(8,128)S(1)} %collective-permute-done.2.refs_0_.refs_1_), channel_id=1, source_target_pairs={{0,8},{4,12},{8,0},{12,4},{16,24},{20,28},{24,16},{28,20},{1,9},{5... | collective-permute-start | bytes 1597448 | tf_op jit(solution)/shard_map/ppermute | solution.py:108
  37.2 20.3 %collective-permute-start.7 = (f32[520,256]{1,0:T(8,128)S(1)}, f32[520,256]{1,0:T(8,128)S(1)}, u32[]{:S(2)}, u32[]{:S(2)}) collective-permute-start(f32[520,256]{1,0:T(8,128)S(1)} %collective-permute-done.1.refs_0_), channel_id=1, source_target_pairs={{0,2},{1,3},{2,0},{3,1},{4,6},{5,7},{6,4},{7,5},{8,10},{9,11},{10,... | collective-permute-start | bytes 1597448 | tf_op jit(solution)/shard_map/ppermute | solution.py:108
  37.6 19.9 %collective-permute-start.6 = (f32[520,256]{1,0:T(8,128)S(1)}, f32[520,256]{1,0:T(8,128)S(1)}, u32[]{:S(2)}, u32[]{:S(2)}) collective-permute-start(f32[520,256]{1,0:T(8,128)S(1)} %collective-permute-done.1.refs_0_), channel_id=1, source_target_pairs={{0,1},{1,0},{2,3},{3,2},{4,5},{5,4},{6,7},{7,6},{8,9},{9,8},{10,11... | collective-permute-start | bytes 1597448 | tf_op jit(solution)/shard_map/ppermute | solution.py:108
  50.5 3.7 %collective-permute-start.9 = (f32[4,4,512]{2,1,0:T(4,128)S(1)}, f32[4,4,512]{2,1,0:T(4,128)S(1)}, u32[]{:S(2)}, u32[]{:S(2)}) collective-permute-start(f32[4,4,512]{2,1,0:T(4,128)S(1)} %get-tuple-element.46.refs_0_), channel_id=1, source_target_pairs={{0,1},{1,0},{2,3},{3,2},{4,5},{5,4},{6,7},{7,6},{8,9},{9,8},{10,11... | collective-permute-start | bytes 98312 | tf_op jit(solution)/shard_map/ppermute | solution.py:108
  54.3 3.2 %collective-permute-start.10 = (f32[2,4,4,512]{3,2,1,0:T(4,128)S(1)}, f32[2,4,4,512]{3,2,1,0:T(4,128)S(1)}, u32[]{:S(2)}, u32[]{:S(2)}) collective-permute-start(f32[2,4,4,512]{3,2,1,0:T(4,128)S(1)} %pad_maximum_fusion), channel_id=1, source_target_pairs={{0,2},{1,3},{2,0},{3,1},{4,6},{5,7},{6,4},{7,5},{8,10},{9,11},{10,... | collective-permute-start | bytes 196616 | tf_op jit(solution)/shard_map/ppermute | solution.py:108
  58.6 7.2 %collective-permute-start.14 = (f32[2,4,512]{2,1,0:T(4,128)S(1)}, f32[2,4,512]{2,1,0:T(4,128)S(1)}, u32[]{:S(2)}, u32[]{:S(2)}) collective-permute-start(f32[2,4,512]{2,1,0:T(4,128)S(1)} %get-tuple-element.58.weight.refs_4_), channel_id=1, source_target_pairs={{0,8},{4,12},{8,0},{12,4},{16,24},{20,28},{24,16},{28,20},{1,9},{5... | collective-permute-start | bytes 49160 | tf_op jit(solution)/shard_map/ppermute | solution.py:108
  65.9 6.5 %collective-permute-start.15 = (f32[2,2,4,512]{3,2,1,0:T(4,128)S(1)}, f32[2,2,4,512]{3,2,1,0:T(4,128)S(1)}, u32[]{:S(2)}, u32[]{:S(2)}) collective-permute-start(f32[2,2,4,512]{3,2,1,0:T(4,128)S(1)} %maximum_add_fusion.1), channel_id=1, source_target_pairs={{0,16},{4,20},{8,24},{12,28},{16,0},{20,4},{24,8},{28,12},{1,17},{... | collective-permute-start | bytes 98312 | tf_op jit(solution)/shard_map/ppermute | solution.py:108
  71.1 11.4 %collective-permute-start.12 = (f32[512,256]{1,0:T(8,128)S(1)}, f32[512,256]{1,0:T(8,128)S(1)}, u32[]{:S(2)}, u32[]{:S(2)}) collective-permute-start(f32[512,256]{1,0:T(8,128)S(1)} %get-tuple-element.57), channel_id=1, source_target_pairs={{0,1},{1,0},{2,3},{3,2},{4,5},{5,4},{6,7},{7,6},{8,9},{9,8},{10,11... | collective-permute-start | bytes 1572872 | tf_op jit(solution)/shard_map/ppermute | solution.py:108
  73.7 32.9 %collective-permute-start.19 = (f32[1040,256]{1,0:T(8,128)S(1)}, f32[1040,256]{1,0:T(8,128)S(1)}, u32[]{:S(2)}, u32[]{:S(2)}) collective-permute-start(f32[1040,256]{1,0:T(8,128)S(1)} %maximum_add_fusion), channel_id=1, source_target_pairs={{0,8},{4,12},{8,0},{12,4},{16,24},{20,28},{24,16},{28,20},{1,9},{5... | collective-permute-start | bytes 3194888 | tf_op jit(solution)/shard_map/ppermute | solution.py:108
  77.7 13.7 %collective-permute-start.20 = (f32[520,256]{1,0:T(8,128)S(1)}, f32[520,256]{1,0:T(8,128)S(1)}, u32[]{:S(2)}, u32[]{:S(2)}) collective-permute-start(f32[520,256]{1,0:T(8,128)S(1)} %collective-permute-done.6.refs_1_), channel_id=1, source_target_pairs={{0,2},{1,3},{2,0},{3,1},{4,6},{5,7},{6,4},{7,5},{8,10},{9,11},{10,... | collective-permute-start | bytes 1597448 | tf_op jit(solution)/shard_map/ppermute | solution.py:108
  81.0 14.2 %collective-permute-start.16 = (f32[520,256]{1,0:T(8,128)S(1)}, f32[520,256]{1,0:T(8,128)S(1)}, u32[]{:S(2)}, u32[]{:S(2)}) collective-permute-start(f32[520,256]{1,0:T(8,128)S(1)} %collective-permute-done.8.refs_0_), channel_id=1, source_target_pairs={{0,1},{1,0},{2,3},{3,2},{4,5},{5,4},{6,7},{7,6},{8,9},{9,8},{10,11... | collective-permute-start | bytes 1597448 | tf_op jit(solution)/shard_map/ppermute | solution.py:108
  81.0 25.4 %collective-permute-start.11 = (f32[512,256]{1,0:T(8,128)S(1)}, f32[512,256]{1,0:T(8,128)S(1)}, u32[]{:S(2)}, u32[]{:S(2)}) collective-permute-start(f32[512,256]{1,0:T(8,128)S(1)} %get-tuple-element.55), channel_id=1, source_target_pairs={{0,1},{1,0},{2,3},{3,2},{4,5},{5,4},{6,7},{7,6},{8,9},{9,8},{10,11... | collective-permute-start | bytes 1572872 | tf_op jit(solution)/shard_map/ppermute | solution.py:108
  82.5 23.9 %collective-permute-start.13 = (f32[512,256]{1,0:T(8,128)S(1)}, f32[512,256]{1,0:T(8,128)S(1)}, u32[]{:S(2)}, u32[]{:S(2)}) collective-permute-start(f32[512,256]{1,0:T(8,128)S(1)} %add.31), channel_id=1, source_target_pairs={{0,2},{1,3},{2,0},{3,1},{4,6},{5,7},{6,4},{7,5},{8,10},{9,11},{10,... | collective-permute-start | bytes 1572872 | tf_op jit(solution)/shard_map/ppermute | solution.py:108
  91.4 22.9 %collective-permute-start.17 = (f32[520,256]{1,0:T(8,128)S(1)}, f32[520,256]{1,0:T(8,128)S(1)}, u32[]{:S(2)}, u32[]{:S(2)}) collective-permute-start(f32[520,256]{1,0:T(8,128)S(1)} %collective-permute-done.8.refs_0_), channel_id=1, source_target_pairs={{0,2},{1,3},{2,0},{3,1},{4,6},{5,7},{6,4},{7,5},{8,10},{9,11},{10,... | collective-permute-start | bytes 1597448 | tf_op jit(solution)/shard_map/ppermute | solution.py:108
  95.2 30.2 %collective-permute-start.18 = (f32[520,256]{1,0:T(8,128)S(1)}, f32[520,256]{1,0:T(8,128)S(1)}, u32[]{:S(2)}, u32[]{:S(2)}) collective-permute-start(f32[520,256]{1,0:T(8,128)S(1)} %collective-permute-done.16.refs_1_), channel_id=1, source_target_pairs={{0,2},{1,3},{2,0},{3,1},{4,6},{5,7},{6,4},{7,5},{8,10},{9,11},{10,... | collective-permute-start | bytes 1597448 | tf_op jit(solution)/shard_map/ppermute | solution.py:108
  106.5 18.9 %copy-start = (f32[512,256]{1,0:T(8,128)}, f32[512,256]{1,0:T(8,128)S(1)}, u32[]{:S(2)}) copy-start(f32[512,256]{1,0:T(8,128)S(1)} %add_add_fusion.refs_4_) | copy-start | bytes 1572868
  135.1 11.0 %collective-permute-start.21 = (f32[2560,256]{1,0:T(8,128)S(1)}, f32[2560,256]{1,0:T(8,128)S(1)}, u32[]{:S(2)}, u32[]{:S(2)}) collective-permute-start(f32[2560,256]{1,0:T(8,128)S(1)} %get-tuple-element.70), channel_id=1, source_target_pairs={{0,4},{4,0},{8,12},{12,8},{16,20},{20,16},{24,28},{28,24},{1,5},{5... | collective-permute-start | bytes 7864328 | tf_op jit(solution)/shard_map/ppermute | solution.py:108
